TPU v7x, 256 devices: a whole 4x4x8 slice. The times are simulated.
256 devices in a mesh: loop: 16 (over x_hi, y, core), inner: 16 (over z, x_lo).
Axes of the slice: x: 4 (x_hi: 2, x_lo: 2; x = x_hi * 2 + x_lo), y: 4, z: 8, core: 2. Of those that a mesh axis runs over, the one named last changes fastest.
Arguments:
- images: bfloat16 [32768, 1536], P(('loop', 'inner')), may hold values from -0.75 to 0.75
- texts: bfloat16 [32768, 1536], P(('loop', 'inner')), may hold values from -0.75 to 0.75
- labels: int32 [32768], P(('loop', 'inner')), may hold values from 0 to 127
- scale: float32 [1], replicated, may hold values from 1 to 4
- bias: float32 [1], replicated, may hold values from -4 to -1
Outputs:
- loss: float32 [1], replicated
- grad_images: float32 [32768, 1536], P(('loop', 'inner'))
- grad_texts: float32 [32768, 1536], P(('loop', 'inner'))
All inputs are finite; a program needn't handle non-finite values.
Results may differ from a plain program's by a relative error of at most 0.0015.
The roundings to bfloat16 on the way count: a program that leaves them out, or rounds other values in their place, can miss the bound.
Values may be sent and summed in bfloat16 or wider, within the bound.
No kernel may reach another device: no remote copies, remote signals or barrier semaphores. Data moves between devices by JAX's collectives and lax.ppermute only.
A program may use at most 128 MiB of HBM per device.

v0:
```python
import functools
import jax
import jax.numpy as jnp
from jax import lax
from jax.experimental import pallas as pl
from jax.experimental.pallas import tpu as pltpu
from jax.sharding import PartitionSpec as P

AXES = ("loop", "inner")
N_LOOP, N_INNER = 16, 16
N_Z = 8
ROWS = 128
HALF = 64
WIDTH = 1536
CODE_WIDTH = WIDTH + 128
GROUPS = 5
IMAGES = GROUPS * 2 * ROWS
TEXTS = N_Z * ROWS
NEAR = 3 * ROWS
EARLY = 5 * ROWS
LATE = 7 * ROWS
TOP = slice(0, HALF)
BOTTOM = slice(HALF, ROWS)
MIB = 1024 * 1024


def pairs(move):
    out = []
    for loop in range(N_LOOP):
        for inner in range(N_INNER):
            chip, core, z, side = loop // 2, loop % 2, inner // 2, inner % 2
            to_chip, to_core, to_z, to_side = move(chip, core, z, side)
            out.append(
                (
                    loop * N_INNER + inner,
                    ((to_chip % 8) * 2 + to_core) * N_INNER + (to_z % N_Z) * 2 + to_side,
                )
            )
    return out


def across_edge(index, first):
    return index + 1 if index % 2 == first else index - 1


Z_EVEN = pairs(lambda c, k, z, s: (c, k, across_edge(z, 0), s))
Z_ODD = pairs(lambda c, k, z, s: (c, k, across_edge(z, 1), s))
CHIP_EVEN = pairs(lambda c, k, z, s: (across_edge(c, 0), k, z, s))
CHIP_ODD = pairs(lambda c, k, z, s: (across_edge(c, 1), k, z, 1 - s if c % 4 in (0, 3) else s))
SIDE = pairs(lambda c, k, z, s: (c, k, z, 1 - s))
CORE = pairs(lambda c, k, z, s: (c, 1 - k, z, s))
def send(array, route):
    return lax.ppermute(array, AXES, route)


Z_FLIP_4 = pairs(lambda c, k, z, s: (c, k, z ^ 4, s))


def exchange(parts, axis):
    parts = parts.reshape(N_LOOP, 8, 128)
    return lax.all_to_all(parts, axis, 0, 0, tiled=True).reshape(8 * N_LOOP, 128)


def vmem(array):
    return pltpu.with_memory_space_constraint(array, pltpu.VMEM)


VM = pl.BlockSpec(memory_space=pltpu.VMEM)
SM = pl.BlockSpec(memory_space=pltpu.SMEM)


def kernel_call(body, outs, args, scratch=(), aliases=None, flops=0, limit=8, after=(), final=False):
    count = len(args)

    def run(*refs):
        body(*refs[:count], *refs[count + len(after) :])

    place = jax.ShapeDtypeStruct if final else pltpu.VMEM
    return pl.pallas_call(
        run,
        out_shape=tuple(place(s, d) for s, d in outs),
        in_specs=[SM if a.ndim == 1 else VM for a in args] + [pl.BlockSpec(memory_space=pl.ANY)] * len(after),
        out_specs=tuple(SM if len(s) == 1 else VM for s, _ in outs),
        scratch_shapes=list(scratch),
        input_output_aliases=aliases or {},
        compiler_params=pltpu.CompilerParams(vmem_limit_bytes=limit * MIB),
        cost_estimate=pl.CostEstimate(flops=flops, bytes_accessed=0, transcendentals=0),
    )(*[a if a.ndim == 1 or final else vmem(a) for a in args], *after)


def encode(value, code_ref, rows, digits=None):
    top = jnp.max(jnp.abs(value), axis=1, keepdims=True)
    power = jnp.floor(jnp.log2(jnp.maximum(top, 1e-30))) - 13.0
    code = jnp.round(value * jnp.exp2(-power)).astype(jnp.int32)
    code_ref[rows, :WIDTH] = code.astype(jnp.int16)
    added = jnp.broadcast_to(power.astype(jnp.int32), (value.shape[0], 128))
    if digits is not None:
        lane = lax.broadcasted_iota(jnp.int32, added.shape, 1)
        added = jnp.where(lane < 32, added, jnp.broadcast_to(digits, added.shape))
    code_ref[rows, WIDTH:] = added.astype(jnp.int16)


def to_digits(total):
    power = jnp.floor(jnp.log2(jnp.maximum(total, 1e-30))) - 13.0
    scaled = total * jnp.exp2(-power)
    high = jnp.floor(scaled)
    low = jnp.round((scaled - high) * 8192.0)
    lane = lax.broadcasted_iota(jnp.int32, total.shape, 1)
    return jnp.where(lane < 64, power, jnp.where(lane < 96, high, low)).astype(jnp.int32)


def read_digits(code_ref):
    return code_ref[:16, WIDTH:].astype(jnp.int32)[:1, :]


def from_digits(digits):
    power, high, low = (digits[:, at : at + 1].astype(jnp.float32) for at in (32, 64, 96))
    return (high + low * (1.0 / 8192.0)) * jnp.exp2(power)


def decode(code_ref, rows):
    power = code_ref[rows, WIDTH:].astype(jnp.int32).astype(jnp.float32)[:, :1]
    return code_ref[rows, :WIDTH].astype(jnp.int32).astype(jnp.float32) * jnp.exp2(power)


def pair_terms(logits, positive):
    signed = logits if positive is None else jnp.where(positive, -logits, logits)
    small = jnp.exp(-jnp.abs(signed))
    whole = 1.0 + small
    weight = jnp.where(signed >= 0, 1.0, small) / whole
    series = small * (1.0 - small * (0.5 - small * (1.0 / 3.0)))
    loss = jnp.maximum(signed, 0.0) + jnp.where(small < 0.01, series, jnp.log(whole))
    if positive is not None:
        weight = jnp.where(positive, -weight, weight)
    return loss, weight.astype(jnp.bfloat16)


def weigh(text, image_ref, out_ref, base, groups, scale, bias, labels, scores):
    rows = text.shape[0]
    total = jnp.zeros((8, 256), jnp.float32)
    for group in groups:
        columns = slice(group * 256, group * 256 + 256)
        scores[:rows] = lax.dot_general(
            text, image_ref[columns, :], (((1,), (1,)), ((), ())), preferred_element_type=jnp.float32
        )
        for start in range(0, rows, 64):
            logits = scale * scores[start : start + 64] + bias
            positive = None
            if labels is not None and group == 0 and start < ROWS:
                row = start + lax.broadcasted_iota(jnp.int32, (64, 256), 0)
                positive = row == jnp.concatenate([labels, jnp.full_like(labels, -1)], axis=1)
            loss, weight = pair_terms(logits, positive)
            out_ref[base + start : base + start + 64, columns] = weight
            total = total + jnp.sum(loss.reshape(8, 8, 256), axis=0)
    return total[:, :128] + total[:, 128:]


def pass_body(array, out):
    del array, out


def choose_body(place, even0, even1, odd0, odd1, out):
    @pl.when(lax.rem(place[0], 2) == 0)
    def _():
        out[:ROWS, :] = even0[...]
        out[ROWS:, :] = even1[...]

    @pl.when(lax.rem(place[0], 2) != 0)
    def _():
        out[:ROWS, :] = odd0[...]
        out[ROWS:, :] = odd1[...]


def third_body(even, odd, even_out, odd_out):
    even_out[...] = even[HALF:, :]
    odd_out[...] = odd[:HALF, :]


def early_body(scale, bias, labels, *refs):
    images, texts = refs[:8], refs[8:13]
    weights, image_all, text_all, loss, scores = refs[13:]
    for i, ref in enumerate(images):
        image_all[i * ROWS : i * ROWS + ROWS, :] = ref[...]
    for i, ref in enumerate(texts):
        text_all[i * ROWS : i * ROWS + ROWS, :] = ref[...]
    loss[...] = weigh(
        text_all[:EARLY, :], image_all, weights, 0, range(4), scale[0], bias[0], labels[...], scores
    )


def middle_body(scale, bias, even, odd, across, loss_in, weights_in, image_in, text_in, weights, image_all, text_all, loss, scores):
    del weights_in, image_in, text_in
    text_all[EARLY : EARLY + ROWS, :] = even[...]
    text_all[EARLY + ROWS : LATE, :] = odd[...]
    image_all[8 * ROWS :, :] = across[...]
    loss[...] = (
        loss_in[...]
        + weigh(
            text_all[EARLY:LATE, :], image_all, weights, EARLY, range(4), scale[0], bias[0], None, scores
        )
        + weigh(text_all[:LATE, :], image_all, weights, 0, (4,), scale[0], bias[0], None, scores)
    )


def late_body(scale, bias, first, second, image_all, loss_in, weights_in, text_in, weights, text_all, loss, code_even, code_odd, far, scores):
    del weights_in, text_in
    text_all[LATE : LATE + HALF, :] = first[...]
    text_all[LATE + HALF :, :] = second[...]
    total = jnp.sum(
        loss_in[...]
        + weigh(
            text_all[LATE:, :], image_all, weights, LATE, range(GROUPS), scale[0], bias[0], None, scores
        )
    )
    digits = to_digits(jnp.full((1, 128), total, jnp.float32))
    loss[...] = jnp.broadcast_to(from_digits(digits), (8, 128))
    grad = jnp.dot(weights[NEAR:, :], image_all[...], preferred_element_type=jnp.float32)
    far[...] = grad[: 4 * ROWS]
    encode(grad[4 * ROWS : 4 * ROWS + HALF], code_even, TOP, digits)
    encode(grad[2 * ROWS : 2 * ROWS + HALF], code_even, BOTTOM, digits)
    encode(grad[4 * ROWS + HALF :], code_odd, TOP, digits)
    encode(grad[3 * ROWS + HALF : 4 * ROWS], code_odd, BOTTOM, digits)


def text_grad_body(weights, image_all, out):
    out[...] = jnp.dot(
        weights[:NEAR, :], image_all[...], preferred_element_type=jnp.float32
    )


def hop_body(top, bottom, top_part, bottom_part, code, out):
    digits = read_digits(code)
    encode(top_part[top : top + HALF, :] + decode(code, TOP), out, TOP, digits)
    if out.shape[0] > HALF:
        encode(bottom_part[bottom : bottom + HALF, :] + decode(code, BOTTOM), out, BOTTOM, digits)


def text_final_body(scale, part, third_even, third_odd, fourth_even, fourth_odd, out, done):
    done[...] = jnp.zeros((8, 128), jnp.float32)
    out[:HALF, :] = scale[0] * (
        part[:HALF, :] + decode(third_even, BOTTOM) + decode(fourth_odd, TOP)
    )
    out[HALF:, :] = scale[0] * (
        part[HALF:ROWS, :] + decode(third_odd, BOTTOM) + decode(fourth_even, TOP)
    )


def loss_sum(parts):
    total = parts[:8, :]
    for start in range(8, 8 * N_LOOP, 8):
        total = total + parts[start : start + 8, :]
    return total


def loss_ring_body(place, own, opposite, *refs):
    *codes, out = refs
    lane = lax.broadcasted_iota(jnp.int32, (8, 128), 1)
    z = lax.div(place[0], 2)
    step = 1 - 2 * lax.rem(z, 2)
    total = jnp.where(lane == z, own[...], 0.0)
    total = total + jnp.where(lane == lax.rem(z + 4, N_Z), opposite[...], 0.0)
    for i, code in enumerate(codes):
        distance = (i // 2 + 1) * (1 - 2 * (i % 2))
        other = lax.rem(z + step * distance + N_Z, N_Z)
        value = jnp.broadcast_to(from_digits(read_digits(code)), (8, 128))
        total = total + jnp.where(lane == other, value, 0.0)
    out[...] = total


def loss_side_body(one, two, out):
    total = one[...] + two[...]
    for i in range(N_LOOP):
        out[8 * i : 8 * i + 8, :] = total


def loss_final_body(parts, out):
    count = float(N_LOOP * N_INNER * ROWS) * float(GROUPS * N_INNER * ROWS)
    out[0] = jnp.sum(loss_sum(parts)[:1, :]) / count


def image_grad(weights, text_all, group):
    return lax.dot_general(
        weights[:, group * 256 : group * 256 + 256],
        text_all[...],
        (((0,), (0,)), ((), ())),
        preferred_element_type=jnp.float32,
    )


def image_code_body(weights, text_all, *outs):
    for i, group in enumerate((1, 4)):
        grad = image_grad(weights, text_all, group)
        for slot in range(2):
            encode(grad[slot * ROWS : slot * ROWS + ROWS], outs[slot], slice(i * ROWS, i * ROWS + ROWS))


def image_keep_body(weights, text_all, own, even, odd):
    for group, ref in ((0, own), (2, even), (3, odd)):
        ref[...] = image_grad(weights, text_all, group)


def chip_body(slot, place, even, odd, code, even_out, odd_out):
    rows = slice(slot * ROWS, slot * ROWS + ROWS)
    extra = decode(code, slice(ROWS, 2 * ROWS))
    first = (lax.rem(place[0], 2) == 0).astype(jnp.float32)
    encode(even[rows, :] + first * extra, even_out, slice(0, ROWS))
    encode(odd[rows, :] + (1.0 - first) * extra, odd_out, slice(0, ROWS))


def side_body(own, other, one, two, out):
    rows = slice(0, ROWS)
    encode(
        own[ROWS:, :] + decode(other, rows) + decode(one, rows) + decode(two, rows), out, rows
    )


def image_sum_body(own, other, one, two, out):
    rows = slice(0, ROWS)
    out[...] = own[:ROWS, :] + decode(other, rows) + decode(one, rows) + decode(two, rows)


def image_final_body(scale, part, side, out, done):
    done[...] = jnp.zeros((8, 128), jnp.float32)
    out[...] = scale[0] * (part[...] + decode(side, slice(0, ROWS)))


CODE = ((HALF, CODE_WIDTH), jnp.int16)
CODE2 = ((ROWS, CODE_WIDTH), jnp.int16)
CODE4 = ((2 * ROWS, CODE_WIDTH), jnp.int16)
BF, F32 = jnp.bfloat16, jnp.float32
UNIT_FLOPS = 2 * ROWS * ROWS * WIDTH
LOSSES = ((8 * N_LOOP, 128), F32)


def on_device(images, texts, labels, scale, bias):
    loop = lax.axis_index("loop")
    place = (
        2 * lax.div(lax.axis_index("inner"), 2) + lax.rem(loop + lax.div(loop, 2), 2)
    ).reshape(1)
    even_1, odd_1 = send(texts, Z_EVEN), send(texts, Z_ODD)
    own = [images, send(images, SIDE)]
    chip_even, chip_odd = [send(images, CHIP_EVEN)], [send(images, CHIP_ODD)]
    own[1] = kernel_call(
        pass_body, [((ROWS, WIDTH), BF)], [own[1]], aliases={0: 0}, after=[chip_even[0], chip_odd[0]]
    )[0]
    chip_even.append(send(own[1], CHIP_EVEN))
    chip_odd.append(send(own[1], CHIP_ODD))
    even_2, odd_2 = send(odd_1, Z_EVEN), send(even_1, Z_ODD)
    other = [send(a, CORE) for a in own]
    even_3, odd_3 = send(odd_2, Z_EVEN), send(even_2, Z_ODD)
    across = send(
        kernel_call(choose_body, [((2 * ROWS, WIDTH), BF)], [place, *chip_even, *chip_odd])[0], CORE
    )
    weights, image_all, text_all, loss = kernel_call(
        early_body,
        [((TEXTS, IMAGES), BF), ((IMAGES, WIDTH), BF), ((TEXTS, WIDTH), BF), ((8, 128), F32)],
        [scale, bias, labels.reshape(1, ROWS), *own, *other, *chip_even, *chip_odd]
        + [texts, even_1, odd_1, even_2, odd_2],
        scratch=[pltpu.VMEM((EARLY, 256), F32)],
        flops=40 * UNIT_FLOPS,
        limit=16,
    )
    last_even, last_odd = kernel_call(
        third_body, [((HALF, WIDTH), BF)] * 2, [even_3, odd_3], flops=60 * UNIT_FLOPS, after=[loss]
    )
    even_4, odd_4 = send(last_odd, Z_EVEN), send(last_even, Z_ODD)
    weights, image_all, text_all, loss = kernel_call(
        middle_body,
        [((TEXTS, IMAGES), BF), ((IMAGES, WIDTH), BF), ((TEXTS, WIDTH), BF), ((8, 128), F32)],
        [scale, bias, even_3, odd_3, across, loss, weights, image_all, text_all],
        scratch=[pltpu.VMEM((LATE, 256), F32)],
        aliases={6: 0, 7: 1, 8: 2},
        flops=30 * UNIT_FLOPS,
        limit=16,
    )
    weights, text_all, loss, code_even, code_odd, far = kernel_call(
        late_body,
        [((TEXTS, IMAGES), BF), ((TEXTS, WIDTH), BF), ((8, 128), F32), CODE2, CODE2, ((4 * ROWS, WIDTH), F32)],
        [scale, bias, even_4, odd_4, image_all, loss, weights, text_all],
        scratch=[pltpu.VMEM((ROWS, 256), F32)],
        aliases={6: 0, 7: 1},
        flops=40 * UNIT_FLOPS,
        limit=16,
    )
    even_1, odd_1 = send(code_even, Z_EVEN), send(code_odd, Z_ODD)
    opposite = send(loss, Z_FLIP_4)
    codes = kernel_call(
        image_code_body, [CODE4] * 2, [weights, text_all], flops=8 * UNIT_FLOPS, limit=16,
        after=[code_even],
    )
    crossed = [send(code, CORE) for code in codes]
    keep = kernel_call(
        image_keep_body,
        [((256, WIDTH), F32)] * 3,
        [weights, text_all],
        flops=10 * UNIT_FLOPS,
        limit=16,
        after=[codes[0]],
    )

    def hop(way, step, code, out=CODE2, after=(), final=False):
        half = HALF * ((step + way) % 2)
        parts = []
        for at in (step, step - 1):
            if at >= 2:
                parts.append((far, (2 * at - 4 + way) * ROWS + half))
            else:
                parts.append((near, max(2 * at - 1 + way, 0) * ROWS + half))
        (one, top), (two, bottom) = parts
        return kernel_call(
            functools.partial(hop_body, top, bottom), [out], [one, two, code],
            flops=400 * UNIT_FLOPS, final=final, after=after,
        )[0]

    def chip(slot):
        to_even, to_odd = kernel_call(
            functools.partial(chip_body, slot), [CODE2] * 2, [place, keep[1], keep[2], crossed[slot]],
            flops=300 * UNIT_FLOPS,
        )
        return [send(to_even, CHIP_EVEN), send(to_odd, CHIP_ODD)], to_odd

    to_even, to_odd = hop(0, 3, odd_1), hop(1, 3, even_1)
    even_2, odd_2 = send(to_even, Z_EVEN), send(to_odd, Z_ODD)
    returned = [None, None]
    returned[1], mark = chip(1)
    near = kernel_call(
        text_grad_body, [((NEAR, WIDTH), F32)], [weights, image_all], flops=10 * UNIT_FLOPS, limit=16,
        after=[mark],
    )[0]
    returned[0], mark = chip(0)
    to_even, to_odd = hop(0, 2, odd_2), hop(1, 2, even_2)
    even_3, odd_3 = send(to_even, Z_EVEN), send(to_odd, Z_ODD)
    to_side = kernel_call(
        side_body, [CODE2], [keep[0], crossed[1], *returned[1]], final=True, flops=300 * UNIT_FLOPS
    )[0]
    from_side = send(to_side, SIDE)
    to_even, to_odd = hop(0, 1, odd_3, CODE, final=True), hop(1, 1, even_3, CODE, after=[opposite], final=True)
    even_4, odd_4 = send(to_even, Z_EVEN), send(to_odd, Z_ODD)
    image_part = kernel_call(
        image_sum_body, [((ROWS, WIDTH), F32)], [keep[0], crossed[0], *returned[0]]
    )[0]
    loss = kernel_call(
        loss_ring_body,
        [((8, 128), F32)],
        [place, loss, opposite, even_1, odd_1, even_2, odd_2, even_3, odd_3],
        after=[to_odd, image_part],
    )[0]
    grad_images, images_done = kernel_call(
        image_final_body,
        [((ROWS, WIDTH), F32), ((8, 128), F32)],
        [scale, image_part, from_side],
        final=True,
    )
    grad_texts, texts_done = kernel_call(
        text_final_body,
        [((ROWS, WIDTH), F32), ((8, 128), F32)],
        [scale, near, even_3, odd_3, even_4, odd_4],
        final=True,
    )
    parts = kernel_call(
        loss_side_body, [LOSSES], [loss, send(loss, SIDE)], final=True, after=[images_done, texts_done]
    )[0]
    parts = exchange(parts, "loop")
    loss = kernel_call(loss_final_body, [((1,), F32)], [parts], final=True)[0]
    return loss, grad_images, grad_texts


def solution(mesh):
    rows = P(AXES, None)
    return jax.shard_map(
        on_device,
        mesh=mesh,
        in_specs=(rows, rows, P(AXES), P(), P()),
        out_specs=(P(), rows, rows),
        check_vma=False,
    )
```

profile of v0, /device:TPU:1, one launch (start us, length us, event | category | flops | bytes accessed | tf_op | source)
XLA Modules:
  0.0 124.7 jit_solution(3708673876977317932)
XLA Ops:
  0.6 0.0 copy-start.3
  0.7 2.2 %collective-permute-start.7 = (bf16[128,1536]{1,0:T(8,128)(2,1)}, bf16[128,1536]{1,0:T(8,128)(2,1)S(1)}, u32[]{:S(2)}, u32[]{:S(2)}) collective-permute-start(bf16[128,1536]{1,0:T(8,128)(2,1)} %refs_3_.1), channel_id=1, source_target_pairs={{0,32},{1,33},{2,34},{3,35},{4,36},{5,37},{6,38},{7,39},{8,40},{9,... | collective-permute-start | bytes 1179656 | tf_op jit(solution)/shard_map/ppermute | solution.py:53
  2.9 4.1 %collective-permute-start.8 = (bf16[128,1536]{1,0:T(8,128)(2,1)}, bf16[128,1536]{1,0:T(8,128)(2,1)S(1)}, u32[]{:S(2)}, u32[]{:S(2)}) collective-permute-start(bf16[128,1536]{1,0:T(8,128)(2,1)} %refs_3_.1), channel_id=1, source_target_pairs={{0,225},{1,224},{2,227},{3,226},{4,229},{5,228},{6,231},{7,230},{8... | collective-permute-start | bytes 1179656 | tf_op jit(solution)/shard_map/ppermute | solution.py:53
  7.0 0.0 collective-permute-start.6
  7.0 1.6 %collective-permute-start = (bf16[128,1536]{1,0:T(8,128)(2,1)}, bf16[128,1536]{1,0:T(8,128)(2,1)S(1)}, u32[]{:S(2)}, u32[]{:S(2)}) collective-permute-start(bf16[128,1536]{1,0:T(8,128)(2,1)} %refs_11_.1), channel_id=1, source_target_pairs={{0,2},{1,3},{2,0},{3,1},{4,6},{5,7},{6,4},{7,5},{8,10},{9,11},{10,... | collective-permute-start | bytes 1179656 | tf_op jit(solution)/shard_map/ppermute | solution.py:53
  8.6 4.7 %collective-permute-start.3 = (bf16[128,1536]{1,0:T(8,128)(2,1)}, bf16[128,1536]{1,0:T(8,128)(2,1)S(1)}, u32[]{:S(2)}, u32[]{:S(2)}) collective-permute-start(bf16[128,1536]{1,0:T(8,128)(2,1)} %refs_11_.1), channel_id=1, source_target_pairs={{0,14},{1,15},{2,4},{3,5},{4,2},{5,3},{6,8},{7,9},{8,6},{9,7},{10,... | collective-permute-start | bytes 1179656 | tf_op jit(solution)/shard_map/ppermute | solution.py:53
  13.3 2.5 %collective-permute-done.8.refs_2_.refs_9_.refs_3_ = bf16[128,1536]{1,0:T(8,128)(2,1)S(1)} collective-permute-done((bf16[128,1536]{1,0:T(8,128)(2,1)}, bf16[128,1536]{1,0:T(8,128)(2,1)S(1)}, u32[]{:S(2)}, u32[]{:S(2)}) %collective-permute-start.8) | collective-permute-done | bytes 393248 | tf_op jit(solution)/shard_map/ppermute | solution.py:53
  15.8 0.8 collective-permute-done.6.refs_0_
  16.6 3.7 %collective-permute-start.12 = (bf16[128,1536]{1,0:T(8,128)(2,1)S(1)}, bf16[128,1536]{1,0:T(8,128)(2,1)S(1)}, u32[]{:S(2)}, u32[]{:S(2)}) collective-permute-start(bf16[128,1536]{1,0:T(8,128)(2,1)S(1)} %shard_map.76.refs_4_), channel_id=1, source_target_pairs={{0,225},{1,224},{2,227},{3,226},{4,229},{5,228},{6,231},{7,230},{8... | collective-permute-start | bytes 1179656 | tf_op jit(solution)/shard_map/ppermute | solution.py:53
  20.3 5.6 %collective-permute-start.1 = (bf16[128,1536]{1,0:T(8,128)(2,1)S(1)}, bf16[128,1536]{1,0:T(8,128)(2,1)}, u32[]{:S(2)}, u32[]{:S(2)}) collective-permute-start(bf16[128,1536]{1,0:T(8,128)(2,1)S(1)} %collective-permute-done.refs_12_), channel_id=1, source_target_pairs={{0,14},{1,15},{2,4},{3,5},{4,2},{5,3},{6,8},{7,9},{8,6},{9,7},{10,... | collective-permute-start | bytes 1179656 | tf_op jit(solution)/shard_map/ppermute | solution.py:53
  25.8 2.4 %collective-permute-start.9 = (bf16[128,1536]{1,0:T(8,128)(2,1)}, bf16[128,1536]{1,0:T(8,128)(2,1)}, u32[]{:S(2)}, u32[]{:S(2)}) collective-permute-start(bf16[128,1536]{1,0:T(8,128)(2,1)} %refs_3_.1), channel_id=1, source_target_pairs={{0,16},{1,17},{2,18},{3,19},{4,20},{5,21},{6,22},{7,23},{8,24},{9,... | collective-permute-start | bytes 1179656 | tf_op jit(solution)/shard_map/ppermute | solution.py:53
  28.3 0.1 collective-permute-start.10
  28.4 0.1 shard_map.79
  28.4 3.1 %collective-permute-start.15 = (bf16[256,1536]{1,0:T(8,128)(2,1)S(1)}, bf16[256,1536]{1,0:T(8,128)(2,1)S(1)}, u32[]{:S(2)}, u32[]{:S(2)}) collective-permute-start(bf16[256,1536]{1,0:T(8,128)(2,1)S(1)} %shard_map.79), channel_id=1, source_target_pairs={{0,16},{1,17},{2,18},{3,19},{4,20},{5,21},{6,22},{7,23},{8,24},{9,... | collective-permute-start | bytes 2359304 | tf_op jit(solution)/shard_map/ppermute | solution.py:53
  31.6 1.7 %collective-permute-done.1.refs_15_ = bf16[128,1536]{1,0:T(8,128)(2,1)} collective-permute-done((bf16[128,1536]{1,0:T(8,128)(2,1)S(1)}, bf16[128,1536]{1,0:T(8,128)(2,1)}, u32[]{:S(2)}, u32[]{:S(2)}) %collective-permute-start.1) | collective-permute-done | bytes 393248 | tf_op jit(solution)/shard_map/ppermute | solution.py:53
  33.2 0.9 collective-permute-done.4.refs_14_
  34.1 3.7 %collective-permute-start.5 = (bf16[128,1536]{1,0:T(8,128)(2,1)}, bf16[128,1536]{1,0:T(8,128)(2,1)S(1)}, u32[]{:S(2)}, u32[]{:S(2)}) collective-permute-start(bf16[128,1536]{1,0:T(8,128)(2,1)} %collective-permute-done.4.refs_14_), channel_id=1, source_target_pairs={{0,14},{1,15},{2,4},{3,5},{4,2},{5,3},{6,8},{7,9},{8,6},{9,7},{10,... | collective-permute-start | bytes 1179656 | tf_op jit(solution)/shard_map/ppermute | solution.py:53
  39.2 5.3 %shard_map.77 = (bf16[1024,1280]{1,0:T(8,128)(2,1)S(1)}, bf16[1280,1536]{1,0:T(8,128)(2,1)S(1)}, bf16[1024,1536]{1,0:T(8,128)(2,1)S(1)}, f32[8,128]{1,0:T(8,128)S(1)}) custom-call(f32[1]{0:T(128)S(6)} %copy.20.refs_0_, f32[1]{0:T(128)S(6)} %copy.21.refs_1_, s32[1,128]{1,0:T(1,128)S(1)} %bitcast.6, bf16[128,1536]{1,0:T(8,128)(2,1)S(1)} %copy-done.3, ...), custom_call_target="tpu_custom_call" | custom-call | flops 2013265920 | tf_op jit(solution)/shard_map/pallas_call | solution.py:79
  44.6 1.2 collective-permute-done.5.refs_1_.refs_3_
  45.8 0.3 collective-permute-start.13
  46.1 3.4 %collective-permute-start.14 = (bf16[64,1536]{1,0:T(8,128)(2,1)S(1)}, bf16[64,1536]{1,0:T(8,128)(2,1)S(1)}, u32[]{:S(2)}, u32[]{:S(2)}) collective-permute-start(bf16[64,1536]{1,0:T(8,128)(2,1)S(1)} %get-tuple-element.34), channel_id=1, source_target_pairs={{0,14},{1,15},{2,4},{3,5},{4,2},{5,3},{6,8},{7,9},{8,6},{9,7},{10,... | collective-permute-start | bytes 589832 | tf_op jit(solution)/shard_map/ppermute | solution.py:53
  49.5 2.8 %shard_map.80 = (bf16[1024,1280]{1,0:T(8,128)(2,1)S(1)}, bf16[1280,1536]{1,0:T(8,128)(2,1)S(1)}, bf16[1024,1536]{1,0:T(8,128)(2,1)S(1)}, f32[8,128]{1,0:T(8,128)S(1)}) custom-call(f32[1]{0:T(128)S(6)} %copy.20.refs_0_, f32[1]{0:T(128)S(6)} %copy.21.refs_1_, ...), custom_call_target="tpu_custom_call", output_to_operand_aliasing={{0}: (6, {}), {1}: (7, {}), {2}: (8, {})} | custom-call | flops 1509949440 | tf_op jit(solution)/shard_map/pallas_call | solution.py:79
  52.4 0.2 collective-permute-done.14.refs_3_
  52.6 4.3 %shard_map.81 = (bf16[1024,1280]{1,0:T(8,128)(2,1)S(1)}, bf16[1024,1536]{1,0:T(8,128)(2,1)S(1)}, f32[8,128]{1,0:T(8,128)}, s16[128,1664]{1,0:T(8,128)(2,1)S(1)},...) custom-call(f32[1]{0:T(128)S(6)} %copy.20.refs_0_, ...), custom_call_target="tpu_custom_call", output_to_operand_aliasing={{0}: (6, {}), {1}: (7, {})} | custom-call | flops 2013265920 | tf_op jit(solution)/shard_map/pallas_call | solution.py:79
  56.9 2.8 %collective-permute-start.18 = (s16[128,1664]{1,0:T(8,128)(2,1)S(1)}, s16[128,1664]{1,0:T(8,128)(2,1)S(1)}, u32[]{:S(2)}, u32[]{:S(2)}) collective-permute-start(s16[128,1664]{1,0:T(8,128)(2,1)S(1)} %get-tuple-element.44), channel_id=1, source_target_pairs={{0,14},{1,15},{2,4},{3,5},{4,2},{5,3},{6,8},{7,9},{8,6},{9,7},{10,... | collective-permute-start | bytes 1277960 | tf_op jit(solution)/shard_map/ppermute | solution.py:53
  59.7 2.1 %shard_map.84 = (s16[256,1664]{1,0:T(8,128)(2,1)S(1)}, s16[256,1664]{1,0:T(8,128)(2,1)S(1)}) custom-call(bf16[1024,1280]{1,0:T(8,128)(2,1)S(1)} %get-tuple-element.46.refs_0_, bf16[1024,1536]{1,0:T(8,128)(2,1)S(1)} %get-tuple-element.47.refs_1_, s16[128,1664]{1,0:T(8,128)(2,1)S(1)} %get-tuple-element.43.refs_2_), custom_call_target="tpu_custom_call" | custom-call | flops 402653184 | tf_op jit(solution)/shard_map/pallas_call | solution.py:79
  61.8 3.2 %collective-permute-start.21 = (s16[256,1664]{1,0:T(8,128)(2,1)S(1)}, s16[256,1664]{1,0:T(8,128)(2,1)S(1)}, u32[]{:S(2)}, u32[]{:S(2)}) collective-permute-start(s16[256,1664]{1,0:T(8,128)(2,1)S(1)} %get-tuple-element.51), channel_id=1, source_target_pairs={{0,16},{1,17},{2,18},{3,19},{4,20},{5,21},{6,22},{7,23},{8,24},{9,... | collective-permute-start | bytes 2555912 | tf_op jit(solution)/shard_map/ppermute | solution.py:53
  65.0 2.8 %collective-permute-start.16 = (f32[8,128]{1,0:T(8,128)}, f32[8,128]{1,0:T(8,128)}, u32[]{:S(2)}, u32[]{:S(2)}) collective-permute-start(f32[8,128]{1,0:T(8,128)} %get-tuple-element.42.refs_1_), channel_id=1, source_target_pairs={{0,8},{1,9},{2,10},{3,11},{4,12},{5,13},{6,14},{7,15},{8,0},{9,1},... | collective-permute-start | bytes 12296 | tf_op jit(solution)/shard_map/ppermute | solution.py:53
  67.8 0.4 collective-permute-start.24
  68.2 2.6 %shard_map.85 = (f32[256,1536]{1,0:T(8,128)S(1)}, f32[256,1536]{1,0:T(8,128)S(1)}, f32[256,1536]{1,0:T(8,128)S(1)}) custom-call(bf16[1024,1280]{1,0:T(8,128)(2,1)S(1)} %get-tuple-element.46.refs_0_, bf16[1024,1536]{1,0:T(8,128)(2,1)S(1)} %get-tuple-element.47.refs_1_, s16[256,1664]{1,0:T(8,128)(2,1)S(1)} %get-tuple-element.48.refs_2_), custom_call_target="tpu_custom_call" | custom-call | flops 503316480 | tf_op jit(solution)/shard_map/pallas_call | solution.py:79
  70.8 0.0 copy-start
  70.8 0.3 shard_map.82
  71.1 0.5 copy-done
  71.6 0.3 collective-permute-start.19
  71.9 0.3 shard_map.83
  72.1 2.8 %collective-permute-start.20 = (s16[128,1664]{1,0:T(8,128)(2,1)S(1)}, s16[128,1664]{1,0:T(8,128)(2,1)S(1)}, u32[]{:S(2)}, u32[]{:S(2)}) collective-permute-start(s16[128,1664]{1,0:T(8,128)(2,1)S(1)} %shard_map.83), channel_id=1, source_target_pairs={{0,14},{1,15},{2,4},{3,5},{4,2},{5,3},{6,8},{7,9},{8,6},{9,7},{10,... | collective-permute-start | bytes 1277960 | tf_op jit(solution)/shard_map/ppermute | solution.py:53
  74.9 0.5 shard_map.86
  75.4 0.1 collective-permute-start.28
  75.5 4.3 %collective-permute-start.29 = (s16[128,1664]{1,0:T(8,128)(2,1)S(1)}, s16[128,1664]{1,0:T(8,128)(2,1)S(1)}, u32[]{:S(2)}, u32[]{:S(2)}) collective-permute-start(s16[128,1664]{1,0:T(8,128)(2,1)S(1)} %get-tuple-element.52.refs_2_), channel_id=1, source_target_pairs={{0,225},{1,224},{2,227},{3,226},{4,229},{5,228},{6,231},{7,230},{8... | collective-permute-start | bytes 1277960 | tf_op jit(solution)/shard_map/ppermute | solution.py:53
  79.8 0.5 shard_map.91
  80.2 1.7 %shard_map.87.refs_1_.refs_0_ = f32[384,1536]{1,0:T(8,128)S(1)} custom-call(bf16[1024,1280]{1,0:T(8,128)(2,1)S(1)} %get-tuple-element.46.refs_0_, bf16[1280,1536]{1,0:T(8,128)(2,1)S(1)} %get-tuple-element.38.refs_4_.refs_1_, s16[128,1664]{1,0:T(8,128)(2,1)S(1)} %get-tuple-element.52.refs_2_), custom_call_target="tpu_custom_call" | custom-call | flops 503316480 | tf_op jit(solution)/shard_map/pallas_call | solution.py:79
  81.9 1.0 collective-permute-done.19.refs_2_.refs_5_
  82.8 0.3 shard_map.89
  83.1 1.3 %collective-permute-done.20.refs_2_.refs_6_ = s16[128,1664]{1,0:T(8,128)(2,1)S(1)} collective-permute-done((s16[128,1664]{1,0:T(8,128)(2,1)S(1)}, s16[128,1664]{1,0:T(8,128)(2,1)S(1)}, u32[]{:S(2)}, u32[]{:S(2)}) %collective-permute-start.20) | collective-permute-done | bytes 426016 | tf_op jit(solution)/shard_map/ppermute | solution.py:53
  84.4 4.3 %collective-permute-start.26 = (s16[128,1664]{1,0:T(8,128)(2,1)S(1)}, s16[128,1664]{1,0:T(8,128)(2,1)S(1)}, u32[]{:S(2)}, u32[]{:S(2)}) collective-permute-start(s16[128,1664]{1,0:T(8,128)(2,1)S(1)} %get-tuple-element.55), channel_id=1, source_target_pairs={{0,225},{1,224},{2,227},{3,226},{4,229},{5,228},{6,231},{7,230},{8... | collective-permute-start | bytes 1277960 | tf_op jit(solution)/shard_map/ppermute | solution.py:53
  88.8 0.3 shard_map.88
  89.1 2.6 %collective-permute-start.23 = (s16[128,1664]{1,0:T(8,128)(2,1)S(1)}, s16[128,1664]{1,0:T(8,128)(2,1)S(1)}, u32[]{:S(2)}, u32[]{:S(2)}) collective-permute-start(s16[128,1664]{1,0:T(8,128)(2,1)S(1)} %shard_map.89), channel_id=1, source_target_pairs={{0,14},{1,15},{2,4},{3,5},{4,2},{5,3},{6,8},{7,9},{8,6},{9,7},{10,... | collective-permute-start | bytes 1277960 | tf_op jit(solution)/shard_map/ppermute | solution.py:53
  91.7 0.4 shard_map.94
  92.1 7.9 %collective-permute-done.23.refs_8_.refs_2_.refs_3_ = s16[128,1664]{1,0:T(8,128)(2,1)S(1)} collective-permute-done((s16[128,1664]{1,0:T(8,128)(2,1)S(1)}, s16[128,1664]{1,0:T(8,128)(2,1)S(1)}, u32[]{:S(2)}, u32[]{:S(2)}) %collective-permute-start.23) | collective-permute-done | bytes 426016 | tf_op jit(solution)/shard_map/ppermute | solution.py:53
  100.0 0.2 shard_map.96
  100.3 0.1 collective-permute-start.31
  100.4 0.7 collective-permute-done.22.refs_2_.refs_7_
  101.1 0.2 shard_map.90.refs_9_
  101.4 0.0 copy-start.1
  101.4 1.9 %collective-permute-start.32 = (s16[64,1664]{1,0:T(8,128)(2,1)S(1)}, s16[64,1664]{1,0:T(8,128)(2,1)S(1)}, u32[]{:S(2)}, u32[]{:S(2)}) collective-permute-start(s16[64,1664]{1,0:T(8,128)(2,1)S(1)} %shard_map.90.refs_9_), channel_id=1, source_target_pairs={{0,14},{1,15},{2,4},{3,5},{4,2},{5,3},{6,8},{7,9},{8,6},{9,7},{10,... | collective-permute-start | bytes 638984 | tf_op jit(solution)/shard_map/ppermute | solution.py:53
  103.3 0.4 shard_map.92.refs_10_.refs_1_
  103.7 0.9 shard_map.93.refs_0_
  104.6 1.5 %collective-permute-start.27 = (f32[8,128]{1,0:T(8,128)S(1)}, f32[8,128]{1,0:T(8,128)S(1)}, u32[]{:S(2)}, u32[]{:S(2)}) collective-permute-start(f32[8,128]{1,0:T(8,128)S(1)} %shard_map.93.refs_0_), channel_id=1, source_target_pairs={{0,1},{1,0},{2,3},{3,2},{4,5},{5,4},{6,7},{7,6},{8,9},{9,8},{10,11... | collective-permute-start | bytes 12296 | tf_op jit(solution)/shard_map/ppermute | solution.py:53
  106.1 1.2 collective-permute-done.32.refs_5_
  107.4 1.2 shard_map.97
  108.5 0.2 collective-permute-done.30.refs_2_
  108.7 1.1 shard_map.95
  109.8 14.1 %all_to_all.5 = f32[16,8,128]{2,1,0:T(8,128)S(1)} all-to-all(f32[16,8,128]{2,1,0:T(8,128)S(1)} %bitcast.4), channel_id=1, replica_groups=mesh['loop'=16,'inner'=16] {'loop'}, dimensions={0} | all-to-all | bytes 131072 | tf_op jit(solution)/shard_map/all_to_all | solution.py:61
  123.9 0.6 shard_map.99
  (37 shorter events, 0.1 us)
Async XLA Ops:
  0.6 38.6 %copy-start.3 = (bf16[128,1536]{1,0:T(8,128)(2,1)S(1)}, bf16[128,1536]{1,0:T(8,128)(2,1)}, u32[]{:S(2)}) copy-start(bf16[128,1536]{1,0:T(8,128)(2,1)} %refs_3_.1) | copy-start | bytes 1179652
  0.6 38.6 %copy-start.2 = (bf16[128,1536]{1,0:T(8,128)(2,1)S(1)}, bf16[128,1536]{1,0:T(8,128)(2,1)}, u32[]{:S(2)}) copy-start(bf16[128,1536]{1,0:T(8,128)(2,1)} %refs_11_.1) | copy-start | bytes 1179652
  0.7 38.6 %copy-start.4 = (s32[128]{0:T(128)S(1)}, s32[128]{0:T(128)}, u32[]{:S(2)}) copy-start(s32[128]{0:T(128)} %param.7) | copy-start | bytes 1540
  0.7 12.6 %collective-permute-start.7 = (bf16[128,1536]{1,0:T(8,128)(2,1)}, bf16[128,1536]{1,0:T(8,128)(2,1)S(1)}, u32[]{:S(2)}, u32[]{:S(2)}) collective-permute-start(bf16[128,1536]{1,0:T(8,128)(2,1)} %refs_3_.1), channel_id=1, source_target_pairs={{0,32},{1,33},{2,34},{3,35},{4,36},{5,37},{6,38},{7,39},{8,40},{9,... | collective-permute-start | bytes 1179656 | tf_op jit(solution)/shard_map/ppermute | solution.py:53
  2.9 12.9 %collective-permute-start.8 = (bf16[128,1536]{1,0:T(8,128)(2,1)}, bf16[128,1536]{1,0:T(8,128)(2,1)S(1)}, u32[]{:S(2)}, u32[]{:S(2)}) collective-permute-start(bf16[128,1536]{1,0:T(8,128)(2,1)} %refs_3_.1), channel_id=1, source_target_pairs={{0,225},{1,224},{2,227},{3,226},{4,229},{5,228},{6,231},{7,230},{8... | collective-permute-start | bytes 1179656 | tf_op jit(solution)/shard_map/ppermute | solution.py:53
  7.0 9.6 %collective-permute-start.6 = (bf16[128,1536]{1,0:T(8,128)(2,1)}, bf16[128,1536]{1,0:T(8,128)(2,1)S(1)}, u32[]{:S(2)}, u32[]{:S(2)}) collective-permute-start(bf16[128,1536]{1,0:T(8,128)(2,1)} %refs_3_.1), channel_id=1, source_target_pairs={{0,1},{1,0},{2,3},{3,2},{4,5},{5,4},{6,7},{7,6},{8,9},{9,8},{10,11... | collective-permute-start | bytes 1179656 | tf_op jit(solution)/shard_map/ppermute | solution.py:53
  7.0 13.3 %collective-permute-start = (bf16[128,1536]{1,0:T(8,128)(2,1)}, bf16[128,1536]{1,0:T(8,128)(2,1)S(1)}, u32[]{:S(2)}, u32[]{:S(2)}) collective-permute-start(bf16[128,1536]{1,0:T(8,128)(2,1)} %refs_11_.1), channel_id=1, source_target_pairs={{0,2},{1,3},{2,0},{3,1},{4,6},{5,7},{6,4},{7,5},{8,10},{9,11},{10,... | collective-permute-start | bytes 1179656 | tf_op jit(solution)/shard_map/ppermute | solution.py:53
  8.6 17.2 %collective-permute-start.3 = (bf16[128,1536]{1,0:T(8,128)(2,1)}, bf16[128,1536]{1,0:T(8,128)(2,1)S(1)}, u32[]{:S(2)}, u32[]{:S(2)}) collective-permute-start(bf16[128,1536]{1,0:T(8,128)(2,1)} %refs_11_.1), channel_id=1, source_target_pairs={{0,14},{1,15},{2,4},{3,5},{4,2},{5,3},{6,8},{7,9},{8,6},{9,7},{10,... | collective-permute-start | bytes 1179656 | tf_op jit(solution)/shard_map/ppermute | solution.py:53
  16.6 11.7 %collective-permute-start.11 = (bf16[128,1536]{1,0:T(8,128)(2,1)S(1)}, bf16[128,1536]{1,0:T(8,128)(2,1)S(1)}, u32[]{:S(2)}, u32[]{:S(2)}) collective-permute-start(bf16[128,1536]{1,0:T(8,128)(2,1)S(1)} %shard_map.76.refs_4_), channel_id=1, source_target_pairs={{0,32},{1,33},{2,34},{3,35},{4,36},{5,37},{6,38},{7,39},{8,40},{9,... | collective-permute-start | bytes 1179656 | tf_op jit(solution)/shard_map/ppermute | solution.py:53
  16.6 11.8 %collective-permute-start.12 = (bf16[128,1536]{1,0:T(8,128)(2,1)S(1)}, bf16[128,1536]{1,0:T(8,128)(2,1)S(1)}, u32[]{:S(2)}, u32[]{:S(2)}) collective-permute-start(bf16[128,1536]{1,0:T(8,128)(2,1)S(1)} %shard_map.76.refs_4_), channel_id=1, source_target_pairs={{0,225},{1,224},{2,227},{3,226},{4,229},{5,228},{6,231},{7,230},{8... | collective-permute-start | bytes 1179656 | tf_op jit(solution)/shard_map/ppermute | solution.py:53
  20.3 13.0 %collective-permute-start.1 = (bf16[128,1536]{1,0:T(8,128)(2,1)S(1)}, bf16[128,1536]{1,0:T(8,128)(2,1)}, u32[]{:S(2)}, u32[]{:S(2)}) collective-permute-start(bf16[128,1536]{1,0:T(8,128)(2,1)S(1)} %collective-permute-done.refs_12_), channel_id=1, source_target_pairs={{0,14},{1,15},{2,4},{3,5},{4,2},{5,3},{6,8},{7,9},{8,6},{9,7},{10,... | collective-permute-start | bytes 1179656 | tf_op jit(solution)/shard_map/ppermute | solution.py:53
  25.8 8.3 %collective-permute-start.4 = (bf16[128,1536]{1,0:T(8,128)(2,1)S(1)}, bf16[128,1536]{1,0:T(8,128)(2,1)}, u32[]{:S(2)}, u32[]{:S(2)}) collective-permute-start(bf16[128,1536]{1,0:T(8,128)(2,1)S(1)} %collective-permute-done.3.refs_13_), channel_id=1, source_target_pairs={{0,2},{1,3},{2,0},{3,1},{4,6},{5,7},{6,4},{7,5},{8,10},{9,11},{10,... | collective-permute-start | bytes 1179656 | tf_op jit(solution)/shard_map/ppermute | solution.py:53
  25.8 13.3 %collective-permute-start.9 = (bf16[128,1536]{1,0:T(8,128)(2,1)}, bf16[128,1536]{1,0:T(8,128)(2,1)}, u32[]{:S(2)}, u32[]{:S(2)}) collective-permute-start(bf16[128,1536]{1,0:T(8,128)(2,1)} %refs_3_.1), channel_id=1, source_target_pairs={{0,16},{1,17},{2,18},{3,19},{4,20},{5,21},{6,22},{7,23},{8,24},{9,... | collective-permute-start | bytes 1179656 | tf_op jit(solution)/shard_map/ppermute | solution.py:53
  28.3 10.9 %collective-permute-start.10 = (bf16[128,1536]{1,0:T(8,128)(2,1)S(1)}, bf16[128,1536]{1,0:T(8,128)(2,1)}, u32[]{:S(2)}, u32[]{:S(2)}) collective-permute-start(bf16[128,1536]{1,0:T(8,128)(2,1)S(1)} %shard_map.76.refs_4_), channel_id=1, source_target_pairs={{0,16},{1,17},{2,18},{3,19},{4,20},{5,21},{6,22},{7,23},{8,24},{9,... | collective-permute-start | bytes 1179656 | tf_op jit(solution)/shard_map/ppermute | solution.py:53
  28.4 21.1 %collective-permute-start.15 = (bf16[256,1536]{1,0:T(8,128)(2,1)S(1)}, bf16[256,1536]{1,0:T(8,128)(2,1)S(1)}, u32[]{:S(2)}, u32[]{:S(2)}) collective-permute-start(bf16[256,1536]{1,0:T(8,128)(2,1)S(1)} %shard_map.79), channel_id=1, source_target_pairs={{0,16},{1,17},{2,18},{3,19},{4,20},{5,21},{6,22},{7,23},{8,24},{9,... | collective-permute-start | bytes 2359304 | tf_op jit(solution)/shard_map/ppermute | solution.py:53
  33.2 11.3 %collective-permute-start.2 = (bf16[128,1536]{1,0:T(8,128)(2,1)}, bf16[128,1536]{1,0:T(8,128)(2,1)S(1)}, u32[]{:S(2)}, u32[]{:S(2)}) collective-permute-start(bf16[128,1536]{1,0:T(8,128)(2,1)} %collective-permute-done.1.refs_15_), channel_id=1, source_target_pairs={{0,2},{1,3},{2,0},{3,1},{4,6},{5,7},{6,4},{7,5},{8,10},{9,11},{10,... | collective-permute-start | bytes 1179656 | tf_op jit(solution)/shard_map/ppermute | solution.py:53
  34.1 11.7 %collective-permute-start.5 = (bf16[128,1536]{1,0:T(8,128)(2,1)}, bf16[128,1536]{1,0:T(8,128)(2,1)S(1)}, u32[]{:S(2)}, u32[]{:S(2)}) collective-permute-start(bf16[128,1536]{1,0:T(8,128)(2,1)} %collective-permute-done.4.refs_14_), channel_id=1, source_target_pairs={{0,14},{1,15},{2,4},{3,5},{4,2},{5,3},{6,8},{7,9},{8,6},{9,7},{10,... | collective-permute-start | bytes 1179656 | tf_op jit(solution)/shard_map/ppermute | solution.py:53
  45.8 6.5 %collective-permute-start.13 = (bf16[64,1536]{1,0:T(8,128)(2,1)S(1)}, bf16[64,1536]{1,0:T(8,128)(2,1)S(1)}, u32[]{:S(2)}, u32[]{:S(2)}) collective-permute-start(bf16[64,1536]{1,0:T(8,128)(2,1)S(1)} %get-tuple-element.33), channel_id=1, source_target_pairs={{0,2},{1,3},{2,0},{3,1},{4,6},{5,7},{6,4},{7,5},{8,10},{9,11},{10,... | collective-permute-start | bytes 589832 | tf_op jit(solution)/shard_map/ppermute | solution.py:53
  46.1 6.5 %collective-permute-start.14 = (bf16[64,1536]{1,0:T(8,128)(2,1)S(1)}, bf16[64,1536]{1,0:T(8,128)(2,1)S(1)}, u32[]{:S(2)}, u32[]{:S(2)}) collective-permute-start(bf16[64,1536]{1,0:T(8,128)(2,1)S(1)} %get-tuple-element.34), channel_id=1, source_target_pairs={{0,14},{1,15},{2,4},{3,5},{4,2},{5,3},{6,8},{7,9},{8,6},{9,7},{10,... | collective-permute-start | bytes 589832 | tf_op jit(solution)/shard_map/ppermute | solution.py:53
  56.9 13.9 %collective-permute-start.18 = (s16[128,1664]{1,0:T(8,128)(2,1)S(1)}, s16[128,1664]{1,0:T(8,128)(2,1)S(1)}, u32[]{:S(2)}, u32[]{:S(2)}) collective-permute-start(s16[128,1664]{1,0:T(8,128)(2,1)S(1)} %get-tuple-element.44), channel_id=1, source_target_pairs={{0,14},{1,15},{2,4},{3,5},{4,2},{5,3},{6,8},{7,9},{8,6},{9,7},{10,... | collective-permute-start | bytes 1277960 | tf_op jit(solution)/shard_map/ppermute | solution.py:53
  59.7 12.2 %collective-permute-start.17 = (s16[128,1664]{1,0:T(8,128)(2,1)S(1)}, s16[128,1664]{1,0:T(8,128)(2,1)S(1)}, u32[]{:S(2)}, u32[]{:S(2)}) collective-permute-start(s16[128,1664]{1,0:T(8,128)(2,1)S(1)} %get-tuple-element.43.refs_2_), channel_id=1, source_target_pairs={{0,2},{1,3},{2,0},{3,1},{4,6},{5,7},{6,4},{7,5},{8,10},{9,11},{10,... | collective-permute-start | bytes 1277960 | tf_op jit(solution)/shard_map/ppermute | solution.py:53
  61.8 13.2 %collective-permute-start.21 = (s16[256,1664]{1,0:T(8,128)(2,1)S(1)}, s16[256,1664]{1,0:T(8,128)(2,1)S(1)}, u32[]{:S(2)}, u32[]{:S(2)}) collective-permute-start(s16[256,1664]{1,0:T(8,128)(2,1)S(1)} %get-tuple-element.51), channel_id=1, source_target_pairs={{0,16},{1,17},{2,18},{3,19},{4,20},{5,21},{6,22},{7,23},{8,24},{9,... | collective-permute-start | bytes 2555912 | tf_op jit(solution)/shard_map/ppermute | solution.py:53
  65.0 35.3 %collective-permute-start.16 = (f32[8,128]{1,0:T(8,128)}, f32[8,128]{1,0:T(8,128)}, u32[]{:S(2)}, u32[]{:S(2)}) collective-permute-start(f32[8,128]{1,0:T(8,128)} %get-tuple-element.42.refs_1_), channel_id=1, source_target_pairs={{0,8},{1,9},{2,10},{3,11},{4,12},{5,13},{6,14},{7,15},{8,0},{9,1},... | collective-permute-start | bytes 12296 | tf_op jit(solution)/shard_map/ppermute | solution.py:53
  67.8 7.7 %collective-permute-start.24 = (s16[256,1664]{1,0:T(8,128)(2,1)S(1)}, s16[256,1664]{1,0:T(8,128)(2,1)S(1)}, u32[]{:S(2)}, u32[]{:S(2)}) collective-permute-start(s16[256,1664]{1,0:T(8,128)(2,1)S(1)} %get-tuple-element.48.refs_2_), channel_id=1, source_target_pairs={{0,16},{1,17},{2,18},{3,19},{4,20},{5,21},{6,22},{7,23},{8,24},{9,... | collective-permute-start | bytes 2555912 | tf_op jit(solution)/shard_map/ppermute | solution.py:53
  70.8 0.8 copy-start
  71.6 11.3 %collective-permute-start.19 = (s16[128,1664]{1,0:T(8,128)(2,1)S(1)}, s16[128,1664]{1,0:T(8,128)(2,1)S(1)}, u32[]{:S(2)}, u32[]{:S(2)}) collective-permute-start(s16[128,1664]{1,0:T(8,128)(2,1)S(1)} %shard_map.82), channel_id=1, source_target_pairs={{0,2},{1,3},{2,0},{3,1},{4,6},{5,7},{6,4},{7,5},{8,10},{9,11},{10,... | collective-permute-start | bytes 1277960 | tf_op jit(solution)/shard_map/ppermute | solution.py:53
  72.1 12.3 %collective-permute-start.20 = (s16[128,1664]{1,0:T(8,128)(2,1)S(1)}, s16[128,1664]{1,0:T(8,128)(2,1)S(1)}, u32[]{:S(2)}, u32[]{:S(2)}) collective-permute-start(s16[128,1664]{1,0:T(8,128)(2,1)S(1)} %shard_map.83), channel_id=1, source_target_pairs={{0,14},{1,15},{2,4},{3,5},{4,2},{5,3},{6,8},{7,9},{8,6},{9,7},{10,... | collective-permute-start | bytes 1277960 | tf_op jit(solution)/shard_map/ppermute | solution.py:53
  75.4 13.7 %collective-permute-start.28 = (s16[128,1664]{1,0:T(8,128)(2,1)S(1)}, s16[128,1664]{1,0:T(8,128)(2,1)S(1)}, u32[]{:S(2)}, u32[]{:S(2)}) collective-permute-start(s16[128,1664]{1,0:T(8,128)(2,1)S(1)} %get-tuple-element.56), channel_id=1, source_target_pairs={{0,32},{1,33},{2,34},{3,35},{4,36},{5,37},{6,38},{7,39},{8,40},{9,... | collective-permute-start | bytes 1277960 | tf_op jit(solution)/shard_map/ppermute | solution.py:53
  75.5 16.2 %collective-permute-start.29 = (s16[128,1664]{1,0:T(8,128)(2,1)S(1)}, s16[128,1664]{1,0:T(8,128)(2,1)S(1)}, u32[]{:S(2)}, u32[]{:S(2)}) collective-permute-start(s16[128,1664]{1,0:T(8,128)(2,1)S(1)} %get-tuple-element.52.refs_2_), channel_id=1, source_target_pairs={{0,225},{1,224},{2,227},{3,226},{4,229},{5,228},{6,231},{7,230},{8... | collective-permute-start | bytes 1277960 | tf_op jit(solution)/shard_map/ppermute | solution.py:53
  82.8 20.5 %collective-permute-start.25 = (s16[128,1664]{1,0:T(8,128)(2,1)S(1)}, s16[128,1664]{1,0:T(8,128)(2,1)S(1)}, u32[]{:S(2)}, u32[]{:S(2)}) collective-permute-start(s16[128,1664]{1,0:T(8,128)(2,1)S(1)} %get-tuple-element.54), channel_id=1, source_target_pairs={{0,32},{1,33},{2,34},{3,35},{4,36},{5,37},{6,38},{7,39},{8,40},{9,... | collective-permute-start | bytes 1277960 | tf_op jit(solution)/shard_map/ppermute | solution.py:53
  84.4 18.9 %collective-permute-start.26 = (s16[128,1664]{1,0:T(8,128)(2,1)S(1)}, s16[128,1664]{1,0:T(8,128)(2,1)S(1)}, u32[]{:S(2)}, u32[]{:S(2)}) collective-permute-start(s16[128,1664]{1,0:T(8,128)(2,1)S(1)} %get-tuple-element.55), channel_id=1, source_target_pairs={{0,225},{1,224},{2,227},{3,226},{4,229},{5,228},{6,231},{7,230},{8... | collective-permute-start | bytes 1277960 | tf_op jit(solution)/shard_map/ppermute | solution.py:53
  89.1 10.9 %collective-permute-start.23 = (s16[128,1664]{1,0:T(8,128)(2,1)S(1)}, s16[128,1664]{1,0:T(8,128)(2,1)S(1)}, u32[]{:S(2)}, u32[]{:S(2)}) collective-permute-start(s16[128,1664]{1,0:T(8,128)(2,1)S(1)} %shard_map.89), channel_id=1, source_target_pairs={{0,14},{1,15},{2,4},{3,5},{4,2},{5,3},{6,8},{7,9},{8,6},{9,7},{10,... | collective-permute-start | bytes 1277960 | tf_op jit(solution)/shard_map/ppermute | solution.py:53
  91.6 9.5 %collective-permute-start.22 = (s16[128,1664]{1,0:T(8,128)(2,1)S(1)}, s16[128,1664]{1,0:T(8,128)(2,1)S(1)}, u32[]{:S(2)}, u32[]{:S(2)}) collective-permute-start(s16[128,1664]{1,0:T(8,128)(2,1)S(1)} %shard_map.88), channel_id=1, source_target_pairs={{0,2},{1,3},{2,0},{3,1},{4,6},{5,7},{6,4},{7,5},{8,10},{9,11},{10,... | collective-permute-start | bytes 1277960 | tf_op jit(solution)/shard_map/ppermute | solution.py:53
  100.0 8.7 %collective-permute-start.30 = (s16[128,1664]{1,0:T(8,128)(2,1)S(1)}, s16[128,1664]{1,0:T(8,128)(2,1)S(1)}, u32[]{:S(2)}, u32[]{:S(2)}) collective-permute-start(s16[128,1664]{1,0:T(8,128)(2,1)S(1)} %shard_map.94), channel_id=1, source_target_pairs={{0,1},{1,0},{2,3},{3,2},{4,5},{5,4},{6,7},{7,6},{8,9},{9,8},{10,11... | collective-permute-start | bytes 1277960 | tf_op jit(solution)/shard_map/ppermute | solution.py:53
  100.3 5.9 %collective-permute-start.31 = (s16[64,1664]{1,0:T(8,128)(2,1)S(1)}, s16[64,1664]{1,0:T(8,128)(2,1)S(1)}, u32[]{:S(2)}, u32[]{:S(2)}) collective-permute-start(s16[64,1664]{1,0:T(8,128)(2,1)S(1)} %shard_map.96), channel_id=1, source_target_pairs={{0,2},{1,3},{2,0},{3,1},{4,6},{5,7},{6,4},{7,5},{8,10},{9,11},{10,... | collective-permute-start | bytes 638984 | tf_op jit(solution)/shard_map/ppermute | solution.py:53
  101.4 2.3 %copy-start.1 = (s16[128,1664]{1,0:T(8,128)(2,1)S(1)}, s16[128,1664]{1,0:T(8,128)(2,1)}, u32[]{:S(2)}) copy-start(s16[128,1664]{1,0:T(8,128)(2,1)} %copy-done) | copy-start | bytes 1277956
  101.4 6.0 %collective-permute-start.32 = (s16[64,1664]{1,0:T(8,128)(2,1)S(1)}, s16[64,1664]{1,0:T(8,128)(2,1)S(1)}, u32[]{:S(2)}, u32[]{:S(2)}) collective-permute-start(s16[64,1664]{1,0:T(8,128)(2,1)S(1)} %shard_map.90.refs_9_), channel_id=1, source_target_pairs={{0,14},{1,15},{2,4},{3,5},{4,2},{5,3},{6,8},{7,9},{8,6},{9,7},{10,... | collective-permute-start | bytes 638984 | tf_op jit(solution)/shard_map/ppermute | solution.py:53
  104.6 5.2 %collective-permute-start.27 = (f32[8,128]{1,0:T(8,128)S(1)}, f32[8,128]{1,0:T(8,128)S(1)}, u32[]{:S(2)}, u32[]{:S(2)}) collective-permute-start(f32[8,128]{1,0:T(8,128)S(1)} %shard_map.93.refs_0_), channel_id=1, source_target_pairs={{0,1},{1,0},{2,3},{3,2},{4,5},{5,4},{6,7},{7,6},{8,9},{9,8},{10,11... | collective-permute-start | bytes 12296 | tf_op jit(solution)/shard_map/ppermute | solution.py:53
where the time goes:
time: 126 us; the launch traced here: 125 us
  starting transfers between devices  62 us (49%)
  Pallas kernels  26 us (21%)
  waiting for transfers between devices  19.7 us (16%)
  blocking collectives  14.1 us (11%)
  between operations  2.42 us (2%)
    ppermute x33, starting transfers between devices, send(): return lax.ppermute(array, AXES, route)  62 us
    pallas_call x24, Pallas kernels, kernel_call(): pl.pallas_call(run, out_shape=tuple((place(s, d) for s, d in outs)), in_s...  26 us
    ppermute x33, waiting for transfers between devices, send(): return lax.ppermute(array, AXES, route)  19.7 us
    all_to_all x1, blocking collectives, exchange(): lax.all_to_all(parts, axis, 0, 0, tiled=True).reshape(8 * N_LOOP, 128)  14.1 us
  transfers between devices with their start and end apart: 33, of which 12 were waited for; matrix products, arithmetic and copies ran while one was open for 0% of the time, Pallas kernels for 17%

commit v1 on v0

--- a/solution.py
+++ b/solution.py
@@ -412,10 +412,10 @@
             flops=400 * UNIT_FLOPS, final=final, after=after,
         )[0]
 
-    def chip(slot):
+    def chip(slot, after=()):
         to_even, to_odd = kernel_call(
             functools.partial(chip_body, slot), [CODE2] * 2, [place, keep[1], keep[2], crossed[slot]],
-            flops=300 * UNIT_FLOPS,
+            flops=300 * UNIT_FLOPS, after=after,
         )
         return [send(to_even, CHIP_EVEN), send(to_odd, CHIP_ODD)], to_odd
 
@@ -425,16 +425,16 @@
     returned[1], mark = chip(1)
     near = kernel_call(
         text_grad_body, [((NEAR, WIDTH), F32)], [weights, image_all], flops=10 * UNIT_FLOPS, limit=16,
-        after=[mark],
-    )[0]
-    returned[0], mark = chip(0)
+        after=[mark, opposite],
+    )[0]
     to_even, to_odd = hop(0, 2, odd_2), hop(1, 2, even_2)
     even_3, odd_3 = send(to_even, Z_EVEN), send(to_odd, Z_ODD)
+    returned[0], mark = chip(0, after=[to_even, to_odd])
     to_side = kernel_call(
         side_body, [CODE2], [keep[0], crossed[1], *returned[1]], final=True, flops=300 * UNIT_FLOPS
     )[0]
     from_side = send(to_side, SIDE)
-    to_even, to_odd = hop(0, 1, odd_3, CODE, final=True), hop(1, 1, even_3, CODE, after=[opposite], final=True)
+    to_even, to_odd = hop(0, 1, odd_3, CODE, final=True), hop(1, 1, even_3, CODE, final=True)
     even_4, odd_4 = send(to_even, Z_EVEN), send(to_odd, Z_ODD)
     image_part = kernel_call(
         image_sum_body, [((ROWS, WIDTH), F32)], [keep[0], crossed[0], *returned[0]]

time: 126 us -> 120 us (0.952)
  waiting for transfers between devices: 19.7 us -> 16.6 us
  starting transfers between devices: 62 us -> 59.5 us
    ppermute x33, waiting for transfers between devices: 19.7 us -> 16.6 us  [send(): return lax.ppermute(array, AXES, route)]
    ppermute x33, starting transfers between devices: 62 us -> 59.5 us  [send(): return lax.ppermute(array, AXES, route)]
  transfers between devices with their start and end apart: 33 -> 33, of which waited for: 12 -> 13; matrix products, arithmetic and copies ran while one was open for 0% -> 0% of each run, Pallas kernels for 17% -> 17%
where the time goes in v1:
time: 120 us
  starting transfers between devices  59.5 us (50%)
  Pallas kernels  25.4 us (21%)
  waiting for transfers between devices  16.6 us (14%)
  blocking collectives  15.3 us (13%)
  between operations  2.45 us (2%)
    ppermute x33, starting transfers between devices, send(): return lax.ppermute(array, AXES, route)  59.5 us
    pallas_call x24, Pallas kernels, kernel_call(): pl.pallas_call(run, out_shape=tuple((place(s, d) for s, d in outs)), in_s...  25.4 us
    ppermute x33, waiting for transfers between devices, send(): return lax.ppermute(array, AXES, route)  16.6 us
    all_to_all x1, blocking collectives, exchange(): lax.all_to_all(parts, axis, 0, 0, tiled=True).reshape(8 * N_LOOP, 128)  15.3 us
  transfers between devices with their start and end apart: 33, of which 13 were waited for; matrix products, arithmetic and copies ran while one was open for 0% of the time, Pallas kernels for 17%

profile of v1, /device:TPU:1, one launch (start us, length us, event | category | flops | bytes accessed | tf_op | source)
XLA Modules:
  0.0 119.8 jit_solution(9885441392972002251)
XLA Ops:
  0.7 2.2 %collective-permute-start.7 = (bf16[128,1536]{1,0:T(8,128)(2,1)}, bf16[128,1536]{1,0:T(8,128)(2,1)S(1)}, u32[]{:S(2)}, u32[]{:S(2)}) collective-permute-start(bf16[128,1536]{1,0:T(8,128)(2,1)} %refs_3_.1), channel_id=1, source_target_pairs={{0,32},{1,33},{2,34},{3,35},{4,36},{5,37},{6,38},{7,39},{8,40},{9,... | collective-permute-start | bytes 1179656 | tf_op jit(solution)/shard_map/ppermute | solution.py:53
  2.9 4.1 %collective-permute-start.8 = (bf16[128,1536]{1,0:T(8,128)(2,1)}, bf16[128,1536]{1,0:T(8,128)(2,1)S(1)}, u32[]{:S(2)}, u32[]{:S(2)}) collective-permute-start(bf16[128,1536]{1,0:T(8,128)(2,1)} %refs_3_.1), channel_id=1, source_target_pairs={{0,225},{1,224},{2,227},{3,226},{4,229},{5,228},{6,231},{7,230},{8... | collective-permute-start | bytes 1179656 | tf_op jit(solution)/shard_map/ppermute | solution.py:53
  7.0 1.6 %collective-permute-start = (bf16[128,1536]{1,0:T(8,128)(2,1)}, bf16[128,1536]{1,0:T(8,128)(2,1)S(1)}, u32[]{:S(2)}, u32[]{:S(2)}) collective-permute-start(bf16[128,1536]{1,0:T(8,128)(2,1)} %refs_11_.1), channel_id=1, source_target_pairs={{0,2},{1,3},{2,0},{3,1},{4,6},{5,7},{6,4},{7,5},{8,10},{9,11},{10,... | collective-permute-start | bytes 1179656 | tf_op jit(solution)/shard_map/ppermute | solution.py:53
  8.6 4.7 %collective-permute-start.3 = (bf16[128,1536]{1,0:T(8,128)(2,1)}, bf16[128,1536]{1,0:T(8,128)(2,1)S(1)}, u32[]{:S(2)}, u32[]{:S(2)}) collective-permute-start(bf16[128,1536]{1,0:T(8,128)(2,1)} %refs_11_.1), channel_id=1, source_target_pairs={{0,14},{1,15},{2,4},{3,5},{4,2},{5,3},{6,8},{7,9},{8,6},{9,7},{10,... | collective-permute-start | bytes 1179656 | tf_op jit(solution)/shard_map/ppermute | solution.py:53
  13.3 2.5 %collective-permute-done.8.refs_2_.refs_9_.refs_3_ = bf16[128,1536]{1,0:T(8,128)(2,1)S(1)} collective-permute-done((bf16[128,1536]{1,0:T(8,128)(2,1)}, bf16[128,1536]{1,0:T(8,128)(2,1)S(1)}, u32[]{:S(2)}, u32[]{:S(2)}) %collective-permute-start.8) | collective-permute-done | bytes 393248 | tf_op jit(solution)/shard_map/ppermute | solution.py:53
  15.8 0.8 collective-permute-done.6.refs_0_
  16.6 3.7 %collective-permute-start.12 = (bf16[128,1536]{1,0:T(8,128)(2,1)S(1)}, bf16[128,1536]{1,0:T(8,128)(2,1)S(1)}, u32[]{:S(2)}, u32[]{:S(2)}) collective-permute-start(bf16[128,1536]{1,0:T(8,128)(2,1)S(1)} %shard_map.76.refs_4_), channel_id=1, source_target_pairs={{0,225},{1,224},{2,227},{3,226},{4,229},{5,228},{6,231},{7,230},{8... | collective-permute-start | bytes 1179656 | tf_op jit(solution)/shard_map/ppermute | solution.py:53
  20.3 5.6 %collective-permute-start.1 = (bf16[128,1536]{1,0:T(8,128)(2,1)S(1)}, bf16[128,1536]{1,0:T(8,128)(2,1)}, u32[]{:S(2)}, u32[]{:S(2)}) collective-permute-start(bf16[128,1536]{1,0:T(8,128)(2,1)S(1)} %collective-permute-done.refs_12_), channel_id=1, source_target_pairs={{0,14},{1,15},{2,4},{3,5},{4,2},{5,3},{6,8},{7,9},{8,6},{9,7},{10,... | collective-permute-start | bytes 1179656 | tf_op jit(solution)/shard_map/ppermute | solution.py:53
  25.8 2.4 %collective-permute-start.9 = (bf16[128,1536]{1,0:T(8,128)(2,1)}, bf16[128,1536]{1,0:T(8,128)(2,1)}, u32[]{:S(2)}, u32[]{:S(2)}) collective-permute-start(bf16[128,1536]{1,0:T(8,128)(2,1)} %refs_3_.1), channel_id=1, source_target_pairs={{0,16},{1,17},{2,18},{3,19},{4,20},{5,21},{6,22},{7,23},{8,24},{9,... | collective-permute-start | bytes 1179656 | tf_op jit(solution)/shard_map/ppermute | solution.py:53
  28.3 0.1 collective-permute-start.10
  28.4 0.1 shard_map.79
  28.4 3.1 %collective-permute-start.15 = (bf16[256,1536]{1,0:T(8,128)(2,1)S(1)}, bf16[256,1536]{1,0:T(8,128)(2,1)S(1)}, u32[]{:S(2)}, u32[]{:S(2)}) collective-permute-start(bf16[256,1536]{1,0:T(8,128)(2,1)S(1)} %shard_map.79), channel_id=1, source_target_pairs={{0,16},{1,17},{2,18},{3,19},{4,20},{5,21},{6,22},{7,23},{8,24},{9,... | collective-permute-start | bytes 2359304 | tf_op jit(solution)/shard_map/ppermute | solution.py:53
  31.6 1.7 %collective-permute-done.1.refs_15_ = bf16[128,1536]{1,0:T(8,128)(2,1)} collective-permute-done((bf16[128,1536]{1,0:T(8,128)(2,1)S(1)}, bf16[128,1536]{1,0:T(8,128)(2,1)}, u32[]{:S(2)}, u32[]{:S(2)}) %collective-permute-start.1) | collective-permute-done | bytes 393248 | tf_op jit(solution)/shard_map/ppermute | solution.py:53
  33.2 0.9 collective-permute-done.4.refs_14_
  34.1 3.7 %collective-permute-start.5 = (bf16[128,1536]{1,0:T(8,128)(2,1)}, bf16[128,1536]{1,0:T(8,128)(2,1)S(1)}, u32[]{:S(2)}, u32[]{:S(2)}) collective-permute-start(bf16[128,1536]{1,0:T(8,128)(2,1)} %collective-permute-done.4.refs_14_), channel_id=1, source_target_pairs={{0,14},{1,15},{2,4},{3,5},{4,2},{5,3},{6,8},{7,9},{8,6},{9,7},{10,... | collective-permute-start | bytes 1179656 | tf_op jit(solution)/shard_map/ppermute | solution.py:53
  39.2 5.3 %shard_map.77 = (bf16[1024,1280]{1,0:T(8,128)(2,1)S(1)}, bf16[1280,1536]{1,0:T(8,128)(2,1)S(1)}, bf16[1024,1536]{1,0:T(8,128)(2,1)S(1)}, f32[8,128]{1,0:T(8,128)S(1)}) custom-call(f32[1]{0:T(128)S(6)} %copy.20.refs_0_, f32[1]{0:T(128)S(6)} %copy.21.refs_1_, s32[1,128]{1,0:T(1,128)S(1)} %bitcast.6, bf16[128,1536]{1,0:T(8,128)(2,1)S(1)} %copy-done.3, ...), custom_call_target="tpu_custom_call" | custom-call | flops 2013265920 | tf_op jit(solution)/shard_map/pallas_call | solution.py:79
  44.6 1.2 %collective-permute-done.5.refs_1_.refs_3_ = bf16[128,1536]{1,0:T(8,128)(2,1)S(1)} collective-permute-done((bf16[128,1536]{1,0:T(8,128)(2,1)}, bf16[128,1536]{1,0:T(8,128)(2,1)S(1)}, u32[]{:S(2)}, u32[]{:S(2)}) %collective-permute-start.5) | collective-permute-done | bytes 393248 | tf_op jit(solution)/shard_map/ppermute | solution.py:53
  45.8 0.3 collective-permute-start.13
  46.1 3.4 %collective-permute-start.14 = (bf16[64,1536]{1,0:T(8,128)(2,1)S(1)}, bf16[64,1536]{1,0:T(8,128)(2,1)S(1)}, u32[]{:S(2)}, u32[]{:S(2)}) collective-permute-start(bf16[64,1536]{1,0:T(8,128)(2,1)S(1)} %get-tuple-element.34), channel_id=1, source_target_pairs={{0,14},{1,15},{2,4},{3,5},{4,2},{5,3},{6,8},{7,9},{8,6},{9,7},{10,... | collective-permute-start | bytes 589832 | tf_op jit(solution)/shard_map/ppermute | solution.py:53
  49.5 2.8 %shard_map.80 = (bf16[1024,1280]{1,0:T(8,128)(2,1)S(1)}, bf16[1280,1536]{1,0:T(8,128)(2,1)S(1)}, bf16[1024,1536]{1,0:T(8,128)(2,1)S(1)}, f32[8,128]{1,0:T(8,128)S(1)}) custom-call(f32[1]{0:T(128)S(6)} %copy.20.refs_0_, f32[1]{0:T(128)S(6)} %copy.21.refs_1_, ...), custom_call_target="tpu_custom_call", output_to_operand_aliasing={{0}: (6, {}), {1}: (7, {}), {2}: (8, {})} | custom-call | flops 1509949440 | tf_op jit(solution)/shard_map/pallas_call | solution.py:79
  52.4 0.2 collective-permute-done.14.refs_3_
  52.6 4.3 %shard_map.81 = (bf16[1024,1280]{1,0:T(8,128)(2,1)S(1)}, bf16[1024,1536]{1,0:T(8,128)(2,1)S(1)}, f32[8,128]{1,0:T(8,128)S(1)}, s16[128,1664]{1,0:T(8,128)(2,1)S(...) custom-call(f32[1]{0:T(128)S(6)} %copy.20.refs_0_, ...), custom_call_target="tpu_custom_call", output_to_operand_aliasing={{0}: (6, {}), {1}: (7, {})} | custom-call | flops 2013265920 | tf_op jit(solution)/shard_map/pallas_call | solution.py:79
  56.9 2.8 %collective-permute-start.18 = (s16[128,1664]{1,0:T(8,128)(2,1)S(1)}, s16[128,1664]{1,0:T(8,128)(2,1)S(1)}, u32[]{:S(2)}, u32[]{:S(2)}) collective-permute-start(s16[128,1664]{1,0:T(8,128)(2,1)S(1)} %get-tuple-element.44), channel_id=1, source_target_pairs={{0,14},{1,15},{2,4},{3,5},{4,2},{5,3},{6,8},{7,9},{8,6},{9,7},{10,... | collective-permute-start | bytes 1277960 | tf_op jit(solution)/shard_map/ppermute | solution.py:53
  59.7 2.1 %shard_map.84 = (s16[256,1664]{1,0:T(8,128)(2,1)S(1)}, s16[256,1664]{1,0:T(8,128)(2,1)S(1)}) custom-call(bf16[1024,1280]{1,0:T(8,128)(2,1)S(1)} %get-tuple-element.46.refs_0_, bf16[1024,1536]{1,0:T(8,128)(2,1)S(1)} %get-tuple-element.47.refs_1_, s16[128,1664]{1,0:T(8,128)(2,1)S(1)} %get-tuple-element.43.refs_2_), custom_call_target="tpu_custom_call" | custom-call | flops 402653184 | tf_op jit(solution)/shard_map/pallas_call | solution.py:79
  61.8 3.2 %collective-permute-start.21 = (s16[256,1664]{1,0:T(8,128)(2,1)S(1)}, s16[256,1664]{1,0:T(8,128)(2,1)S(1)}, u32[]{:S(2)}, u32[]{:S(2)}) collective-permute-start(s16[256,1664]{1,0:T(8,128)(2,1)S(1)} %get-tuple-element.51), channel_id=1, source_target_pairs={{0,16},{1,17},{2,18},{3,19},{4,20},{5,21},{6,22},{7,23},{8,24},{9,... | collective-permute-start | bytes 2555912 | tf_op jit(solution)/shard_map/ppermute | solution.py:53
  65.0 2.8 %collective-permute-start.16 = (f32[8,128]{1,0:T(8,128)S(1)}, f32[8,128]{1,0:T(8,128)S(1)}, u32[]{:S(2)}, u32[]{:S(2)}) collective-permute-start(f32[8,128]{1,0:T(8,128)S(1)} %get-tuple-element.42.refs_1_), channel_id=1, source_target_pairs={{0,8},{1,9},{2,10},{3,11},{4,12},{5,13},{6,14},{7,15},{8,0},{9,1},... | collective-permute-start | bytes 12296 | tf_op jit(solution)/shard_map/ppermute | solution.py:53
  67.8 0.4 collective-permute-start.24
  68.2 2.6 %shard_map.85 = (f32[256,1536]{1,0:T(8,128)S(1)}, f32[256,1536]{1,0:T(8,128)S(1)}, f32[256,1536]{1,0:T(8,128)S(1)}) custom-call(bf16[1024,1280]{1,0:T(8,128)(2,1)S(1)} %get-tuple-element.46.refs_0_, bf16[1024,1536]{1,0:T(8,128)(2,1)S(1)} %get-tuple-element.47.refs_1_, s16[256,1664]{1,0:T(8,128)(2,1)S(1)} %get-tuple-element.48.refs_2_), custom_call_target="tpu_custom_call" | custom-call | flops 503316480 | tf_op jit(solution)/shard_map/pallas_call | solution.py:79
  70.8 0.3 shard_map.82
  71.1 0.5 copy-done
  71.6 0.3 collective-permute-start.19
  71.9 0.3 shard_map.83
  72.1 2.8 %collective-permute-start.20 = (s16[128,1664]{1,0:T(8,128)(2,1)S(1)}, s16[128,1664]{1,0:T(8,128)(2,1)S(1)}, u32[]{:S(2)}, u32[]{:S(2)}) collective-permute-start(s16[128,1664]{1,0:T(8,128)(2,1)S(1)} %shard_map.83), channel_id=1, source_target_pairs={{0,14},{1,15},{2,4},{3,5},{4,2},{5,3},{6,8},{7,9},{8,6},{9,7},{10,... | collective-permute-start | bytes 1277960 | tf_op jit(solution)/shard_map/ppermute | solution.py:53
  74.9 0.5 shard_map.86
  75.4 0.1 collective-permute-start.28
  75.5 4.3 %collective-permute-start.29 = (s16[128,1664]{1,0:T(8,128)(2,1)S(1)}, s16[128,1664]{1,0:T(8,128)(2,1)S(1)}, u32[]{:S(2)}, u32[]{:S(2)}) collective-permute-start(s16[128,1664]{1,0:T(8,128)(2,1)S(1)} %get-tuple-element.52.refs_2_), channel_id=1, source_target_pairs={{0,225},{1,224},{2,227},{3,226},{4,229},{5,228},{6,231},{7,230},{8... | collective-permute-start | bytes 1277960 | tf_op jit(solution)/shard_map/ppermute | solution.py:53
  79.8 1.7 %shard_map.87.refs_1_.refs_0_ = f32[384,1536]{1,0:T(8,128)S(1)} custom-call(bf16[1024,1280]{1,0:T(8,128)(2,1)S(1)} %get-tuple-element.46.refs_0_, bf16[1280,1536]{1,0:T(8,128)(2,1)S(1)} %get-tuple-element.38.refs_4_.refs_1_, s16[128,1664]{1,0:T(8,128)(2,1)S(1)} %get-tuple-element.52.refs_2_, f32[8,128]{1,0:T(8,128)S(1)} %collective-permute-done.16.refs_3_.refs_2_), custom_call_target="tpu_custom_call" | custom-call | flops 503316480 | tf_op jit(solution)/shard_map/pallas_call | solution.py:79
  81.5 1.4 %collective-permute-done.19.refs_2_.refs_5_ = s16[128,1664]{1,0:T(8,128)(2,1)S(1)} collective-permute-done((s16[128,1664]{1,0:T(8,128)(2,1)S(1)}, s16[128,1664]{1,0:T(8,128)(2,1)S(1)}, u32[]{:S(2)}, u32[]{:S(2)}) %collective-permute-start.19) | collective-permute-done | bytes 426016 | tf_op jit(solution)/shard_map/ppermute | solution.py:53
  82.8 0.3 shard_map.89.refs_5_
  83.1 0.9 collective-permute-start.23
  84.0 0.4 collective-permute-done.20.refs_2_.refs_6_
  84.4 0.3 shard_map.88.refs_4_
  84.7 0.1 collective-permute-start.22
  84.8 0.5 shard_map.91
  85.3 0.1 collective-permute-start.25
  85.4 0.7 collective-permute-done.28.refs_2_
  86.1 4.2 %collective-permute-start.26 = (s16[128,1664]{1,0:T(8,128)(2,1)S(1)}, s16[128,1664]{1,0:T(8,128)(2,1)S(1)}, u32[]{:S(2)}, u32[]{:S(2)}) collective-permute-start(s16[128,1664]{1,0:T(8,128)(2,1)S(1)} %get-tuple-element.55), channel_id=1, source_target_pairs={{0,225},{1,224},{2,227},{3,226},{4,229},{5,228},{6,231},{7,230},{8... | collective-permute-start | bytes 1277960 | tf_op jit(solution)/shard_map/ppermute | solution.py:53
  90.3 0.4 shard_map.94
  90.8 0.1 collective-permute-start.30
  90.9 3.9 %collective-permute-done.23.refs_8_.refs_2_.refs_3_ = s16[128,1664]{1,0:T(8,128)(2,1)S(1)} collective-permute-done((s16[128,1664]{1,0:T(8,128)(2,1)S(1)}, s16[128,1664]{1,0:T(8,128)(2,1)S(1)}, u32[]{:S(2)}, u32[]{:S(2)}) %collective-permute-start.23) | collective-permute-done | bytes 426016 | tf_op jit(solution)/shard_map/ppermute | solution.py:53
  94.8 0.2 shard_map.96
  95.0 0.1 collective-permute-start.31
  95.1 0.2 shard_map.90.refs_9_
  95.4 2.4 %collective-permute-start.32 = (s16[64,1664]{1,0:T(8,128)(2,1)S(1)}, s16[64,1664]{1,0:T(8,128)(2,1)S(1)}, u32[]{:S(2)}, u32[]{:S(2)}) collective-permute-start(s16[64,1664]{1,0:T(8,128)(2,1)S(1)} %shard_map.90.refs_9_), channel_id=1, source_target_pairs={{0,14},{1,15},{2,4},{3,5},{4,2},{5,3},{6,8},{7,9},{8,6},{9,7},{10,... | collective-permute-start | bytes 638984 | tf_op jit(solution)/shard_map/ppermute | solution.py:53
  97.8 1.3 %collective-permute-done.26.refs_3_ = s16[128,1664]{1,0:T(8,128)(2,1)S(1)} collective-permute-done((s16[128,1664]{1,0:T(8,128)(2,1)S(1)}, s16[128,1664]{1,0:T(8,128)(2,1)S(1)}, u32[]{:S(2)}, u32[]{:S(2)}) %collective-permute-start.26) | collective-permute-done | bytes 426016 | tf_op jit(solution)/shard_map/ppermute | solution.py:53
  99.2 0.4 shard_map.92.refs_10_.refs_1_
  99.6 0.2 shard_map.93.refs_0_
  99.8 0.1 collective-permute-start.27
  99.9 0.3 collective-permute-done.31.refs_4_
  100.1 1.3 %collective-permute-done.32.refs_5_ = s16[64,1664]{1,0:T(8,128)(2,1)S(1)} collective-permute-done((s16[64,1664]{1,0:T(8,128)(2,1)S(1)}, s16[64,1664]{1,0:T(8,128)(2,1)S(1)}, u32[]{:S(2)}, u32[]{:S(2)}) %collective-permute-start.32) | collective-permute-done | bytes 213024 | tf_op jit(solution)/shard_map/ppermute | solution.py:53
  101.4 1.2 shard_map.97
  102.6 1.1 shard_map.95
  103.6 15.3 %all_to_all.5 = f32[16,8,128]{2,1,0:T(8,128)S(1)} all-to-all(f32[16,8,128]{2,1,0:T(8,128)S(1)} %bitcast.4), channel_id=1, replica_groups=mesh['loop'=16,'inner'=16] {'loop'}, dimensions={0} | all-to-all | bytes 131072 | tf_op jit(solution)/shard_map/all_to_all | solution.py:61
  118.9 0.6 shard_map.99
  (37 shorter events, 0.1 us)
Async XLA Ops:
  0.6 38.6 %copy-start.3 = (bf16[128,1536]{1,0:T(8,128)(2,1)S(1)}, bf16[128,1536]{1,0:T(8,128)(2,1)}, u32[]{:S(2)}) copy-start(bf16[128,1536]{1,0:T(8,128)(2,1)} %refs_3_.1) | copy-start | bytes 1179652
  0.6 38.6 %copy-start.2 = (bf16[128,1536]{1,0:T(8,128)(2,1)S(1)}, bf16[128,1536]{1,0:T(8,128)(2,1)}, u32[]{:S(2)}) copy-start(bf16[128,1536]{1,0:T(8,128)(2,1)} %refs_11_.1) | copy-start | bytes 1179652
  0.7 38.6 %copy-start.4 = (s32[128]{0:T(128)S(1)}, s32[128]{0:T(128)}, u32[]{:S(2)}) copy-start(s32[128]{0:T(128)} %param.7) | copy-start | bytes 1540
  0.7 12.6 %collective-permute-start.7 = (bf16[128,1536]{1,0:T(8,128)(2,1)}, bf16[128,1536]{1,0:T(8,128)(2,1)S(1)}, u32[]{:S(2)}, u32[]{:S(2)}) collective-permute-start(bf16[128,1536]{1,0:T(8,128)(2,1)} %refs_3_.1), channel_id=1, source_target_pairs={{0,32},{1,33},{2,34},{3,35},{4,36},{5,37},{6,38},{7,39},{8,40},{9,... | collective-permute-start | bytes 1179656 | tf_op jit(solution)/shard_map/ppermute | solution.py:53
  2.9 12.9 %collective-permute-start.8 = (bf16[128,1536]{1,0:T(8,128)(2,1)}, bf16[128,1536]{1,0:T(8,128)(2,1)S(1)}, u32[]{:S(2)}, u32[]{:S(2)}) collective-permute-start(bf16[128,1536]{1,0:T(8,128)(2,1)} %refs_3_.1), channel_id=1, source_target_pairs={{0,225},{1,224},{2,227},{3,226},{4,229},{5,228},{6,231},{7,230},{8... | collective-permute-start | bytes 1179656 | tf_op jit(solution)/shard_map/ppermute | solution.py:53
  7.0 9.6 %collective-permute-start.6 = (bf16[128,1536]{1,0:T(8,128)(2,1)}, bf16[128,1536]{1,0:T(8,128)(2,1)S(1)}, u32[]{:S(2)}, u32[]{:S(2)}) collective-permute-start(bf16[128,1536]{1,0:T(8,128)(2,1)} %refs_3_.1), channel_id=1, source_target_pairs={{0,1},{1,0},{2,3},{3,2},{4,5},{5,4},{6,7},{7,6},{8,9},{9,8},{10,11... | collective-permute-start | bytes 1179656 | tf_op jit(solution)/shard_map/ppermute | solution.py:53
  7.0 13.3 %collective-permute-start = (bf16[128,1536]{1,0:T(8,128)(2,1)}, bf16[128,1536]{1,0:T(8,128)(2,1)S(1)}, u32[]{:S(2)}, u32[]{:S(2)}) collective-permute-start(bf16[128,1536]{1,0:T(8,128)(2,1)} %refs_11_.1), channel_id=1, source_target_pairs={{0,2},{1,3},{2,0},{3,1},{4,6},{5,7},{6,4},{7,5},{8,10},{9,11},{10,... | collective-permute-start | bytes 1179656 | tf_op jit(solution)/shard_map/ppermute | solution.py:53
  8.6 17.2 %collective-permute-start.3 = (bf16[128,1536]{1,0:T(8,128)(2,1)}, bf16[128,1536]{1,0:T(8,128)(2,1)S(1)}, u32[]{:S(2)}, u32[]{:S(2)}) collective-permute-start(bf16[128,1536]{1,0:T(8,128)(2,1)} %refs_11_.1), channel_id=1, source_target_pairs={{0,14},{1,15},{2,4},{3,5},{4,2},{5,3},{6,8},{7,9},{8,6},{9,7},{10,... | collective-permute-start | bytes 1179656 | tf_op jit(solution)/shard_map/ppermute | solution.py:53
  16.6 11.7 %collective-permute-start.11 = (bf16[128,1536]{1,0:T(8,128)(2,1)S(1)}, bf16[128,1536]{1,0:T(8,128)(2,1)S(1)}, u32[]{:S(2)}, u32[]{:S(2)}) collective-permute-start(bf16[128,1536]{1,0:T(8,128)(2,1)S(1)} %shard_map.76.refs_4_), channel_id=1, source_target_pairs={{0,32},{1,33},{2,34},{3,35},{4,36},{5,37},{6,38},{7,39},{8,40},{9,... | collective-permute-start | bytes 1179656 | tf_op jit(solution)/shard_map/ppermute | solution.py:53
  16.6 11.8 %collective-permute-start.12 = (bf16[128,1536]{1,0:T(8,128)(2,1)S(1)}, bf16[128,1536]{1,0:T(8,128)(2,1)S(1)}, u32[]{:S(2)}, u32[]{:S(2)}) collective-permute-start(bf16[128,1536]{1,0:T(8,128)(2,1)S(1)} %shard_map.76.refs_4_), channel_id=1, source_target_pairs={{0,225},{1,224},{2,227},{3,226},{4,229},{5,228},{6,231},{7,230},{8... | collective-permute-start | bytes 1179656 | tf_op jit(solution)/shard_map/ppermute | solution.py:53
  20.3 13.0 %collective-permute-start.1 = (bf16[128,1536]{1,0:T(8,128)(2,1)S(1)}, bf16[128,1536]{1,0:T(8,128)(2,1)}, u32[]{:S(2)}, u32[]{:S(2)}) collective-permute-start(bf16[128,1536]{1,0:T(8,128)(2,1)S(1)} %collective-permute-done.refs_12_), channel_id=1, source_target_pairs={{0,14},{1,15},{2,4},{3,5},{4,2},{5,3},{6,8},{7,9},{8,6},{9,7},{10,... | collective-permute-start | bytes 1179656 | tf_op jit(solution)/shard_map/ppermute | solution.py:53
  25.8 8.3 %collective-permute-start.4 = (bf16[128,1536]{1,0:T(8,128)(2,1)S(1)}, bf16[128,1536]{1,0:T(8,128)(2,1)}, u32[]{:S(2)}, u32[]{:S(2)}) collective-permute-start(bf16[128,1536]{1,0:T(8,128)(2,1)S(1)} %collective-permute-done.3.refs_13_), channel_id=1, source_target_pairs={{0,2},{1,3},{2,0},{3,1},{4,6},{5,7},{6,4},{7,5},{8,10},{9,11},{10,... | collective-permute-start | bytes 1179656 | tf_op jit(solution)/shard_map/ppermute | solution.py:53
  25.8 13.3 %collective-permute-start.9 = (bf16[128,1536]{1,0:T(8,128)(2,1)}, bf16[128,1536]{1,0:T(8,128)(2,1)}, u32[]{:S(2)}, u32[]{:S(2)}) collective-permute-start(bf16[128,1536]{1,0:T(8,128)(2,1)} %refs_3_.1), channel_id=1, source_target_pairs={{0,16},{1,17},{2,18},{3,19},{4,20},{5,21},{6,22},{7,23},{8,24},{9,... | collective-permute-start | bytes 1179656 | tf_op jit(solution)/shard_map/ppermute | solution.py:53
  28.3 10.9 %collective-permute-start.10 = (bf16[128,1536]{1,0:T(8,128)(2,1)S(1)}, bf16[128,1536]{1,0:T(8,128)(2,1)}, u32[]{:S(2)}, u32[]{:S(2)}) collective-permute-start(bf16[128,1536]{1,0:T(8,128)(2,1)S(1)} %shard_map.76.refs_4_), channel_id=1, source_target_pairs={{0,16},{1,17},{2,18},{3,19},{4,20},{5,21},{6,22},{7,23},{8,24},{9,... | collective-permute-start | bytes 1179656 | tf_op jit(solution)/shard_map/ppermute | solution.py:53
  28.4 21.1 %collective-permute-start.15 = (bf16[256,1536]{1,0:T(8,128)(2,1)S(1)}, bf16[256,1536]{1,0:T(8,128)(2,1)S(1)}, u32[]{:S(2)}, u32[]{:S(2)}) collective-permute-start(bf16[256,1536]{1,0:T(8,128)(2,1)S(1)} %shard_map.79), channel_id=1, source_target_pairs={{0,16},{1,17},{2,18},{3,19},{4,20},{5,21},{6,22},{7,23},{8,24},{9,... | collective-permute-start | bytes 2359304 | tf_op jit(solution)/shard_map/ppermute | solution.py:53
  33.2 11.3 %collective-permute-start.2 = (bf16[128,1536]{1,0:T(8,128)(2,1)}, bf16[128,1536]{1,0:T(8,128)(2,1)S(1)}, u32[]{:S(2)}, u32[]{:S(2)}) collective-permute-start(bf16[128,1536]{1,0:T(8,128)(2,1)} %collective-permute-done.1.refs_15_), channel_id=1, source_target_pairs={{0,2},{1,3},{2,0},{3,1},{4,6},{5,7},{6,4},{7,5},{8,10},{9,11},{10,... | collective-permute-start | bytes 1179656 | tf_op jit(solution)/shard_map/ppermute | solution.py:53
  34.1 11.7 %collective-permute-start.5 = (bf16[128,1536]{1,0:T(8,128)(2,1)}, bf16[128,1536]{1,0:T(8,128)(2,1)S(1)}, u32[]{:S(2)}, u32[]{:S(2)}) collective-permute-start(bf16[128,1536]{1,0:T(8,128)(2,1)} %collective-permute-done.4.refs_14_), channel_id=1, source_target_pairs={{0,14},{1,15},{2,4},{3,5},{4,2},{5,3},{6,8},{7,9},{8,6},{9,7},{10,... | collective-permute-start | bytes 1179656 | tf_op jit(solution)/shard_map/ppermute | solution.py:53
  45.8 6.5 %collective-permute-start.13 = (bf16[64,1536]{1,0:T(8,128)(2,1)S(1)}, bf16[64,1536]{1,0:T(8,128)(2,1)S(1)}, u32[]{:S(2)}, u32[]{:S(2)}) collective-permute-start(bf16[64,1536]{1,0:T(8,128)(2,1)S(1)} %get-tuple-element.33), channel_id=1, source_target_pairs={{0,2},{1,3},{2,0},{3,1},{4,6},{5,7},{6,4},{7,5},{8,10},{9,11},{10,... | collective-permute-start | bytes 589832 | tf_op jit(solution)/shard_map/ppermute | solution.py:53
  46.1 6.5 %collective-permute-start.14 = (bf16[64,1536]{1,0:T(8,128)(2,1)S(1)}, bf16[64,1536]{1,0:T(8,128)(2,1)S(1)}, u32[]{:S(2)}, u32[]{:S(2)}) collective-permute-start(bf16[64,1536]{1,0:T(8,128)(2,1)S(1)} %get-tuple-element.34), channel_id=1, source_target_pairs={{0,14},{1,15},{2,4},{3,5},{4,2},{5,3},{6,8},{7,9},{8,6},{9,7},{10,... | collective-permute-start | bytes 589832 | tf_op jit(solution)/shard_map/ppermute | solution.py:53
  56.9 13.9 %collective-permute-start.18 = (s16[128,1664]{1,0:T(8,128)(2,1)S(1)}, s16[128,1664]{1,0:T(8,128)(2,1)S(1)}, u32[]{:S(2)}, u32[]{:S(2)}) collective-permute-start(s16[128,1664]{1,0:T(8,128)(2,1)S(1)} %get-tuple-element.44), channel_id=1, source_target_pairs={{0,14},{1,15},{2,4},{3,5},{4,2},{5,3},{6,8},{7,9},{8,6},{9,7},{10,... | collective-permute-start | bytes 1277960 | tf_op jit(solution)/shard_map/ppermute | solution.py:53
  59.7 12.2 %collective-permute-start.17 = (s16[128,1664]{1,0:T(8,128)(2,1)S(1)}, s16[128,1664]{1,0:T(8,128)(2,1)S(1)}, u32[]{:S(2)}, u32[]{:S(2)}) collective-permute-start(s16[128,1664]{1,0:T(8,128)(2,1)S(1)} %get-tuple-element.43.refs_2_), channel_id=1, source_target_pairs={{0,2},{1,3},{2,0},{3,1},{4,6},{5,7},{6,4},{7,5},{8,10},{9,11},{10,... | collective-permute-start | bytes 1277960 | tf_op jit(solution)/shard_map/ppermute | solution.py:53
  61.8 13.2 %collective-permute-start.21 = (s16[256,1664]{1,0:T(8,128)(2,1)S(1)}, s16[256,1664]{1,0:T(8,128)(2,1)S(1)}, u32[]{:S(2)}, u32[]{:S(2)}) collective-permute-start(s16[256,1664]{1,0:T(8,128)(2,1)S(1)} %get-tuple-element.51), channel_id=1, source_target_pairs={{0,16},{1,17},{2,18},{3,19},{4,20},{5,21},{6,22},{7,23},{8,24},{9,... | collective-permute-start | bytes 2555912 | tf_op jit(solution)/shard_map/ppermute | solution.py:53
  65.0 10.5 %collective-permute-start.16 = (f32[8,128]{1,0:T(8,128)S(1)}, f32[8,128]{1,0:T(8,128)S(1)}, u32[]{:S(2)}, u32[]{:S(2)}) collective-permute-start(f32[8,128]{1,0:T(8,128)S(1)} %get-tuple-element.42.refs_1_), channel_id=1, source_target_pairs={{0,8},{1,9},{2,10},{3,11},{4,12},{5,13},{6,14},{7,15},{8,0},{9,1},... | collective-permute-start | bytes 12296 | tf_op jit(solution)/shard_map/ppermute | solution.py:53
  67.8 17.0 %collective-permute-start.24 = (s16[256,1664]{1,0:T(8,128)(2,1)S(1)}, s16[256,1664]{1,0:T(8,128)(2,1)S(1)}, u32[]{:S(2)}, u32[]{:S(2)}) collective-permute-start(s16[256,1664]{1,0:T(8,128)(2,1)S(1)} %get-tuple-element.48.refs_2_), channel_id=1, source_target_pairs={{0,16},{1,17},{2,18},{3,19},{4,20},{5,21},{6,22},{7,23},{8,24},{9,... | collective-permute-start | bytes 2555912 | tf_op jit(solution)/shard_map/ppermute | solution.py:53
  70.8 0.8 copy-start
  71.6 11.3 %collective-permute-start.19 = (s16[128,1664]{1,0:T(8,128)(2,1)S(1)}, s16[128,1664]{1,0:T(8,128)(2,1)S(1)}, u32[]{:S(2)}, u32[]{:S(2)}) collective-permute-start(s16[128,1664]{1,0:T(8,128)(2,1)S(1)} %shard_map.82), channel_id=1, source_target_pairs={{0,2},{1,3},{2,0},{3,1},{4,6},{5,7},{6,4},{7,5},{8,10},{9,11},{10,... | collective-permute-start | bytes 1277960 | tf_op jit(solution)/shard_map/ppermute | solution.py:53
  72.1 12.3 %collective-permute-start.20 = (s16[128,1664]{1,0:T(8,128)(2,1)S(1)}, s16[128,1664]{1,0:T(8,128)(2,1)S(1)}, u32[]{:S(2)}, u32[]{:S(2)}) collective-permute-start(s16[128,1664]{1,0:T(8,128)(2,1)S(1)} %shard_map.83), channel_id=1, source_target_pairs={{0,14},{1,15},{2,4},{3,5},{4,2},{5,3},{6,8},{7,9},{8,6},{9,7},{10,... | collective-permute-start | bytes 1277960 | tf_op jit(solution)/shard_map/ppermute | solution.py:53
  75.4 10.7 %collective-permute-start.28 = (s16[128,1664]{1,0:T(8,128)(2,1)S(1)}, s16[128,1664]{1,0:T(8,128)(2,1)S(1)}, u32[]{:S(2)}, u32[]{:S(2)}) collective-permute-start(s16[128,1664]{1,0:T(8,128)(2,1)S(1)} %get-tuple-element.56), channel_id=1, source_target_pairs={{0,32},{1,33},{2,34},{3,35},{4,36},{5,37},{6,38},{7,39},{8,40},{9,... | collective-permute-start | bytes 1277960 | tf_op jit(solution)/shard_map/ppermute | solution.py:53
  75.5 14.8 %collective-permute-start.29 = (s16[128,1664]{1,0:T(8,128)(2,1)S(1)}, s16[128,1664]{1,0:T(8,128)(2,1)S(1)}, u32[]{:S(2)}, u32[]{:S(2)}) collective-permute-start(s16[128,1664]{1,0:T(8,128)(2,1)S(1)} %get-tuple-element.52.refs_2_), channel_id=1, source_target_pairs={{0,225},{1,224},{2,227},{3,226},{4,229},{5,228},{6,231},{7,230},{8... | collective-permute-start | bytes 1277960 | tf_op jit(solution)/shard_map/ppermute | solution.py:53
  83.1 11.7 %collective-permute-start.23 = (s16[128,1664]{1,0:T(8,128)(2,1)S(1)}, s16[128,1664]{1,0:T(8,128)(2,1)S(1)}, u32[]{:S(2)}, u32[]{:S(2)}) collective-permute-start(s16[128,1664]{1,0:T(8,128)(2,1)S(1)} %shard_map.89.refs_5_), channel_id=1, source_target_pairs={{0,14},{1,15},{2,4},{3,5},{4,2},{5,3},{6,8},{7,9},{8,6},{9,7},{10,... | collective-permute-start | bytes 1277960 | tf_op jit(solution)/shard_map/ppermute | solution.py:53
  84.7 10.4 %collective-permute-start.22 = (s16[128,1664]{1,0:T(8,128)(2,1)S(1)}, s16[128,1664]{1,0:T(8,128)(2,1)S(1)}, u32[]{:S(2)}, u32[]{:S(2)}) collective-permute-start(s16[128,1664]{1,0:T(8,128)(2,1)S(1)} %shard_map.88.refs_4_), channel_id=1, source_target_pairs={{0,2},{1,3},{2,0},{3,1},{4,6},{5,7},{6,4},{7,5},{8,10},{9,11},{10,... | collective-permute-start | bytes 1277960 | tf_op jit(solution)/shard_map/ppermute | solution.py:53
  85.3 12.5 %collective-permute-start.25 = (s16[128,1664]{1,0:T(8,128)(2,1)S(1)}, s16[128,1664]{1,0:T(8,128)(2,1)S(1)}, u32[]{:S(2)}, u32[]{:S(2)}) collective-permute-start(s16[128,1664]{1,0:T(8,128)(2,1)S(1)} %get-tuple-element.54), channel_id=1, source_target_pairs={{0,32},{1,33},{2,34},{3,35},{4,36},{5,37},{6,38},{7,39},{8,40},{9,... | collective-permute-start | bytes 1277960 | tf_op jit(solution)/shard_map/ppermute | solution.py:53
  86.1 13.0 %collective-permute-start.26 = (s16[128,1664]{1,0:T(8,128)(2,1)S(1)}, s16[128,1664]{1,0:T(8,128)(2,1)S(1)}, u32[]{:S(2)}, u32[]{:S(2)}) collective-permute-start(s16[128,1664]{1,0:T(8,128)(2,1)S(1)} %get-tuple-element.55), channel_id=1, source_target_pairs={{0,225},{1,224},{2,227},{3,226},{4,229},{5,228},{6,231},{7,230},{8... | collective-permute-start | bytes 1277960 | tf_op jit(solution)/shard_map/ppermute | solution.py:53
  90.8 11.8 %collective-permute-start.30 = (s16[128,1664]{1,0:T(8,128)(2,1)S(1)}, s16[128,1664]{1,0:T(8,128)(2,1)S(1)}, u32[]{:S(2)}, u32[]{:S(2)}) collective-permute-start(s16[128,1664]{1,0:T(8,128)(2,1)S(1)} %shard_map.94), channel_id=1, source_target_pairs={{0,1},{1,0},{2,3},{3,2},{4,5},{5,4},{6,7},{7,6},{8,9},{9,8},{10,11... | collective-permute-start | bytes 1277960 | tf_op jit(solution)/shard_map/ppermute | solution.py:53
  95.0 5.1 %collective-permute-start.31 = (s16[64,1664]{1,0:T(8,128)(2,1)S(1)}, s16[64,1664]{1,0:T(8,128)(2,1)S(1)}, u32[]{:S(2)}, u32[]{:S(2)}) collective-permute-start(s16[64,1664]{1,0:T(8,128)(2,1)S(1)} %shard_map.96), channel_id=1, source_target_pairs={{0,2},{1,3},{2,0},{3,1},{4,6},{5,7},{6,4},{7,5},{8,10},{9,11},{10,... | collective-permute-start | bytes 638984 | tf_op jit(solution)/shard_map/ppermute | solution.py:53
  95.4 4.2 %copy-start.1 = (s16[128,1664]{1,0:T(8,128)(2,1)S(1)}, s16[128,1664]{1,0:T(8,128)(2,1)}, u32[]{:S(2)}) copy-start(s16[128,1664]{1,0:T(8,128)(2,1)} %copy-done) | copy-start | bytes 1277956
  95.4 6.0 %collective-permute-start.32 = (s16[64,1664]{1,0:T(8,128)(2,1)S(1)}, s16[64,1664]{1,0:T(8,128)(2,1)S(1)}, u32[]{:S(2)}, u32[]{:S(2)}) collective-permute-start(s16[64,1664]{1,0:T(8,128)(2,1)S(1)} %shard_map.90.refs_9_), channel_id=1, source_target_pairs={{0,14},{1,15},{2,4},{3,5},{4,2},{5,3},{6,8},{7,9},{8,6},{9,7},{10,... | collective-permute-start | bytes 638984 | tf_op jit(solution)/shard_map/ppermute | solution.py:53
  99.8 3.9 %collective-permute-start.27 = (f32[8,128]{1,0:T(8,128)S(1)}, f32[8,128]{1,0:T(8,128)S(1)}, u32[]{:S(2)}, u32[]{:S(2)}) collective-permute-start(f32[8,128]{1,0:T(8,128)S(1)} %shard_map.93.refs_0_), channel_id=1, source_target_pairs={{0,1},{1,0},{2,3},{3,2},{4,5},{5,4},{6,7},{7,6},{8,9},{9,8},{10,11... | collective-permute-start | bytes 12296 | tf_op jit(solution)/shard_map/ppermute | solution.py:53

commit v2 on v1

--- a/solution.py
+++ b/solution.py
@@ -451,14 +451,14 @@
         [scale, image_part, from_side],
         final=True,
     )
-    grad_texts, texts_done = kernel_call(
+    grad_texts, _ = kernel_call(
         text_final_body,
         [((ROWS, WIDTH), F32), ((8, 128), F32)],
         [scale, near, even_3, odd_3, even_4, odd_4],
         final=True,
     )
     parts = kernel_call(
-        loss_side_body, [LOSSES], [loss, send(loss, SIDE)], final=True, after=[images_done, texts_done]
+        loss_side_body, [LOSSES], [loss, send(loss, SIDE)], final=True, after=[images_done]
     )[0]
     parts = exchange(parts, "loop")
     loss = kernel_call(loss_final_body, [((1,), F32)], [parts], final=True)[0]

time: 120 us -> 120 us (level)
  blocking collectives: 15.3 us -> 0 us
  starting transfers between devices: 59.5 us -> 67.1 us
  waiting for transfers between devices: 16.6 us -> 22.2 us
  Pallas kernels: 25.4 us -> 27.6 us
    all_to_all x1 -> x0, blocking collectives: 15.3 us -> none  [exchange(): lax.all_to_all(parts, axis, 0, 0, tiled=True).reshape(8 * N_LOOP, 128)]
    all_to_all x0 -> x1, starting transfers between devices: none -> 8.34 us  [exchange(): lax.all_to_all(parts, axis, 0, 0, tiled=True).reshape(8 * N_LOOP, 128)]
    all_to_all x0 -> x1, waiting for transfers between devices: none -> 5.13 us  [exchange(): lax.all_to_all(parts, axis, 0, 0, tiled=True).reshape(8 * N_LOOP, 128)]
    pallas_call x24, Pallas kernels: 25.4 us -> 27.6 us  [kernel_call(): pl.pallas_call(run, out_shape=tuple((place(s, d) for s, d in outs)), in_s...]
  transfers between devices with their start and end apart: 33 -> 34, of which waited for: 13 -> 14; matrix products, arithmetic and copies ran while one was open for 0% -> 0% of each run, Pallas kernels for 17% -> 19%
where the time goes in v2:
time: 120 us
  starting transfers between devices  67.1 us (56%)
  Pallas kernels  27.6 us (23%)
  waiting for transfers between devices  22.2 us (18%)
  between operations  2.44 us (2%)
    ppermute x33, starting transfers between devices, send(): return lax.ppermute(array, AXES, route)  58.8 us
    pallas_call x24, Pallas kernels, kernel_call(): pl.pallas_call(run, out_shape=tuple((place(s, d) for s, d in outs)), in_s...  27.6 us
    ppermute x33, waiting for transfers between devices, send(): return lax.ppermute(array, AXES, route)  17.1 us
    all_to_all x1, starting transfers between devices, exchange(): lax.all_to_all(parts, axis, 0, 0, tiled=True).reshape(8 * N_LOOP, 128)  8.34 us
    all_to_all x1, waiting for transfers between devices, exchange(): lax.all_to_all(parts, axis, 0, 0, tiled=True).reshape(8 * N_LOOP, 128)  5.13 us
  transfers between devices with their start and end apart: 34, of which 14 were waited for; matrix products, arithmetic and copies ran while one was open for 0% of the time, Pallas kernels for 19%

profile of v2, /device:TPU:1, one launch (start us, length us, event | category | flops | bytes accessed | tf_op | source)
XLA Modules:
  0.0 119.9 jit_solution(3854634522688495490)
XLA Ops:
  0.7 2.2 %collective-permute-start.7 = (bf16[128,1536]{1,0:T(8,128)(2,1)}, bf16[128,1536]{1,0:T(8,128)(2,1)S(1)}, u32[]{:S(2)}, u32[]{:S(2)}) collective-permute-start(bf16[128,1536]{1,0:T(8,128)(2,1)} %refs_3_.1), channel_id=1, source_target_pairs={{0,32},{1,33},{2,34},{3,35},{4,36},{5,37},{6,38},{7,39},{8,40},{9,... | collective-permute-start | bytes 1179656 | tf_op jit(solution)/shard_map/ppermute | solution.py:53
  2.9 4.1 %collective-permute-start.8 = (bf16[128,1536]{1,0:T(8,128)(2,1)}, bf16[128,1536]{1,0:T(8,128)(2,1)S(1)}, u32[]{:S(2)}, u32[]{:S(2)}) collective-permute-start(bf16[128,1536]{1,0:T(8,128)(2,1)} %refs_3_.1), channel_id=1, source_target_pairs={{0,225},{1,224},{2,227},{3,226},{4,229},{5,228},{6,231},{7,230},{8... | collective-permute-start | bytes 1179656 | tf_op jit(solution)/shard_map/ppermute | solution.py:53
  7.0 1.6 %collective-permute-start = (bf16[128,1536]{1,0:T(8,128)(2,1)}, bf16[128,1536]{1,0:T(8,128)(2,1)S(1)}, u32[]{:S(2)}, u32[]{:S(2)}) collective-permute-start(bf16[128,1536]{1,0:T(8,128)(2,1)} %refs_11_.1), channel_id=1, source_target_pairs={{0,2},{1,3},{2,0},{3,1},{4,6},{5,7},{6,4},{7,5},{8,10},{9,11},{10,... | collective-permute-start | bytes 1179656 | tf_op jit(solution)/shard_map/ppermute | solution.py:53
  8.6 4.7 %collective-permute-start.3 = (bf16[128,1536]{1,0:T(8,128)(2,1)}, bf16[128,1536]{1,0:T(8,128)(2,1)S(1)}, u32[]{:S(2)}, u32[]{:S(2)}) collective-permute-start(bf16[128,1536]{1,0:T(8,128)(2,1)} %refs_11_.1), channel_id=1, source_target_pairs={{0,14},{1,15},{2,4},{3,5},{4,2},{5,3},{6,8},{7,9},{8,6},{9,7},{10,... | collective-permute-start | bytes 1179656 | tf_op jit(solution)/shard_map/ppermute | solution.py:53
  13.3 2.5 %collective-permute-done.8.refs_2_.refs_9_.refs_3_ = bf16[128,1536]{1,0:T(8,128)(2,1)S(1)} collective-permute-done((bf16[128,1536]{1,0:T(8,128)(2,1)}, bf16[128,1536]{1,0:T(8,128)(2,1)S(1)}, u32[]{:S(2)}, u32[]{:S(2)}) %collective-permute-start.8) | collective-permute-done | bytes 393248 | tf_op jit(solution)/shard_map/ppermute | solution.py:53
  15.8 0.8 collective-permute-done.6.refs_0_
  16.6 3.7 %collective-permute-start.12 = (bf16[128,1536]{1,0:T(8,128)(2,1)S(1)}, bf16[128,1536]{1,0:T(8,128)(2,1)S(1)}, u32[]{:S(2)}, u32[]{:S(2)}) collective-permute-start(bf16[128,1536]{1,0:T(8,128)(2,1)S(1)} %shard_map.76.refs_4_), channel_id=1, source_target_pairs={{0,225},{1,224},{2,227},{3,226},{4,229},{5,228},{6,231},{7,230},{8... | collective-permute-start | bytes 1179656 | tf_op jit(solution)/shard_map/ppermute | solution.py:53
  20.3 5.6 %collective-permute-start.1 = (bf16[128,1536]{1,0:T(8,128)(2,1)S(1)}, bf16[128,1536]{1,0:T(8,128)(2,1)}, u32[]{:S(2)}, u32[]{:S(2)}) collective-permute-start(bf16[128,1536]{1,0:T(8,128)(2,1)S(1)} %collective-permute-done.refs_12_), channel_id=1, source_target_pairs={{0,14},{1,15},{2,4},{3,5},{4,2},{5,3},{6,8},{7,9},{8,6},{9,7},{10,... | collective-permute-start | bytes 1179656 | tf_op jit(solution)/shard_map/ppermute | solution.py:53
  25.8 2.4 %collective-permute-start.9 = (bf16[128,1536]{1,0:T(8,128)(2,1)}, bf16[128,1536]{1,0:T(8,128)(2,1)}, u32[]{:S(2)}, u32[]{:S(2)}) collective-permute-start(bf16[128,1536]{1,0:T(8,128)(2,1)} %refs_3_.1), channel_id=1, source_target_pairs={{0,16},{1,17},{2,18},{3,19},{4,20},{5,21},{6,22},{7,23},{8,24},{9,... | collective-permute-start | bytes 1179656 | tf_op jit(solution)/shard_map/ppermute | solution.py:53
  28.3 0.1 collective-permute-start.10
  28.4 3.1 %collective-permute-start.15 = (bf16[256,1536]{1,0:T(8,128)(2,1)S(1)}, bf16[256,1536]{1,0:T(8,128)(2,1)S(1)}, u32[]{:S(2)}, u32[]{:S(2)}) collective-permute-start(bf16[256,1536]{1,0:T(8,128)(2,1)S(1)} %shard_map.79), channel_id=1, source_target_pairs={{0,16},{1,17},{2,18},{3,19},{4,20},{5,21},{6,22},{7,23},{8,24},{9,... | collective-permute-start | bytes 2359304 | tf_op jit(solution)/shard_map/ppermute | solution.py:53
  31.6 1.7 %collective-permute-done.1.refs_15_ = bf16[128,1536]{1,0:T(8,128)(2,1)} collective-permute-done((bf16[128,1536]{1,0:T(8,128)(2,1)S(1)}, bf16[128,1536]{1,0:T(8,128)(2,1)}, u32[]{:S(2)}, u32[]{:S(2)}) %collective-permute-start.1) | collective-permute-done | bytes 393248 | tf_op jit(solution)/shard_map/ppermute | solution.py:53
  33.2 0.9 collective-permute-done.4.refs_14_
  34.1 3.7 %collective-permute-start.5 = (bf16[128,1536]{1,0:T(8,128)(2,1)}, bf16[128,1536]{1,0:T(8,128)(2,1)S(1)}, u32[]{:S(2)}, u32[]{:S(2)}) collective-permute-start(bf16[128,1536]{1,0:T(8,128)(2,1)} %collective-permute-done.4.refs_14_), channel_id=1, source_target_pairs={{0,14},{1,15},{2,4},{3,5},{4,2},{5,3},{6,8},{7,9},{8,6},{9,7},{10,... | collective-permute-start | bytes 1179656 | tf_op jit(solution)/shard_map/ppermute | solution.py:53
  39.2 5.3 %shard_map.77 = (bf16[1024,1280]{1,0:T(8,128)(2,1)S(1)}, bf16[1280,1536]{1,0:T(8,128)(2,1)S(1)}, bf16[1024,1536]{1,0:T(8,128)(2,1)S(1)}, f32[8,128]{1,0:T(8,128)S(1)}) custom-call(f32[1]{0:T(128)S(6)} %copy.20.refs_0_, f32[1]{0:T(128)S(6)} %copy.21.refs_1_, s32[1,128]{1,0:T(1,128)S(1)} %bitcast.5, bf16[128,1536]{1,0:T(8,128)(2,1)S(1)} %copy-done.3, ...), custom_call_target="tpu_custom_call" | custom-call | flops 2013265920 | tf_op jit(solution)/shard_map/pallas_call | solution.py:79
  44.6 1.2 %collective-permute-done.5.refs_1_.refs_3_ = bf16[128,1536]{1,0:T(8,128)(2,1)S(1)} collective-permute-done((bf16[128,1536]{1,0:T(8,128)(2,1)}, bf16[128,1536]{1,0:T(8,128)(2,1)S(1)}, u32[]{:S(2)}, u32[]{:S(2)}) %collective-permute-start.5) | collective-permute-done | bytes 393248 | tf_op jit(solution)/shard_map/ppermute | solution.py:53
  45.8 0.3 collective-permute-start.13
  46.1 3.4 %collective-permute-start.14 = (bf16[64,1536]{1,0:T(8,128)(2,1)S(1)}, bf16[64,1536]{1,0:T(8,128)(2,1)S(1)}, u32[]{:S(2)}, u32[]{:S(2)}) collective-permute-start(bf16[64,1536]{1,0:T(8,128)(2,1)S(1)} %get-tuple-element.33), channel_id=1, source_target_pairs={{0,14},{1,15},{2,4},{3,5},{4,2},{5,3},{6,8},{7,9},{8,6},{9,7},{10,... | collective-permute-start | bytes 589832 | tf_op jit(solution)/shard_map/ppermute | solution.py:53
  49.5 2.8 %shard_map.80 = (bf16[1024,1280]{1,0:T(8,128)(2,1)S(1)}, bf16[1280,1536]{1,0:T(8,128)(2,1)S(1)}, bf16[1024,1536]{1,0:T(8,128)(2,1)S(1)}, f32[8,128]{1,0:T(8,128)S(1)}) custom-call(f32[1]{0:T(128)S(6)} %copy.20.refs_0_, f32[1]{0:T(128)S(6)} %copy.21.refs_1_, ...), custom_call_target="tpu_custom_call", output_to_operand_aliasing={{0}: (6, {}), {1}: (7, {}), {2}: (8, {})} | custom-call | flops 1509949440 | tf_op jit(solution)/shard_map/pallas_call | solution.py:79
  52.4 0.2 collective-permute-done.14.refs_3_
  52.6 4.3 %shard_map.81 = (bf16[1024,1280]{1,0:T(8,128)(2,1)S(1)}, bf16[1024,1536]{1,0:T(8,128)(2,1)S(1)}, f32[8,128]{1,0:T(8,128)S(1)}, s16[128,1664]{1,0:T(8,128)(2,1)S(...) custom-call(f32[1]{0:T(128)S(6)} %copy.20.refs_0_, ...), custom_call_target="tpu_custom_call", output_to_operand_aliasing={{0}: (6, {}), {1}: (7, {})} | custom-call | flops 2013265920 | tf_op jit(solution)/shard_map/pallas_call | solution.py:79
  56.9 2.8 %collective-permute-start.18 = (s16[128,1664]{1,0:T(8,128)(2,1)S(1)}, s16[128,1664]{1,0:T(8,128)(2,1)S(1)}, u32[]{:S(2)}, u32[]{:S(2)}) collective-permute-start(s16[128,1664]{1,0:T(8,128)(2,1)S(1)} %get-tuple-element.43), channel_id=1, source_target_pairs={{0,14},{1,15},{2,4},{3,5},{4,2},{5,3},{6,8},{7,9},{8,6},{9,7},{10,... | collective-permute-start | bytes 1277960 | tf_op jit(solution)/shard_map/ppermute | solution.py:53
  59.7 2.1 %shard_map.84 = (s16[256,1664]{1,0:T(8,128)(2,1)S(1)}, s16[256,1664]{1,0:T(8,128)(2,1)S(1)}) custom-call(bf16[1024,1280]{1,0:T(8,128)(2,1)S(1)} %get-tuple-element.45.refs_0_, bf16[1024,1536]{1,0:T(8,128)(2,1)S(1)} %get-tuple-element.46.refs_1_, s16[128,1664]{1,0:T(8,128)(2,1)S(1)} %get-tuple-element.42.refs_2_), custom_call_target="tpu_custom_call" | custom-call | flops 402653184 | tf_op jit(solution)/shard_map/pallas_call | solution.py:79
  61.8 3.2 %collective-permute-start.21 = (s16[256,1664]{1,0:T(8,128)(2,1)S(1)}, s16[256,1664]{1,0:T(8,128)(2,1)S(1)}, u32[]{:S(2)}, u32[]{:S(2)}) collective-permute-start(s16[256,1664]{1,0:T(8,128)(2,1)S(1)} %get-tuple-element.50), channel_id=1, source_target_pairs={{0,16},{1,17},{2,18},{3,19},{4,20},{5,21},{6,22},{7,23},{8,24},{9,... | collective-permute-start | bytes 2555912 | tf_op jit(solution)/shard_map/ppermute | solution.py:53
  65.0 2.8 %collective-permute-start.16 = (f32[8,128]{1,0:T(8,128)S(1)}, f32[8,128]{1,0:T(8,128)S(1)}, u32[]{:S(2)}, u32[]{:S(2)}) collective-permute-start(f32[8,128]{1,0:T(8,128)S(1)} %get-tuple-element.41.refs_1_), channel_id=1, source_target_pairs={{0,8},{1,9},{2,10},{3,11},{4,12},{5,13},{6,14},{7,15},{8,0},{9,1},... | collective-permute-start | bytes 12296 | tf_op jit(solution)/shard_map/ppermute | solution.py:53
  67.8 0.4 collective-permute-start.24
  68.2 2.6 %shard_map.85 = (f32[256,1536]{1,0:T(8,128)S(1)}, f32[256,1536]{1,0:T(8,128)S(1)}, f32[256,1536]{1,0:T(8,128)S(1)}) custom-call(bf16[1024,1280]{1,0:T(8,128)(2,1)S(1)} %get-tuple-element.45.refs_0_, bf16[1024,1536]{1,0:T(8,128)(2,1)S(1)} %get-tuple-element.46.refs_1_, s16[256,1664]{1,0:T(8,128)(2,1)S(1)} %get-tuple-element.47.refs_2_), custom_call_target="tpu_custom_call" | custom-call | flops 503316480 | tf_op jit(solution)/shard_map/pallas_call | solution.py:79
  70.8 0.3 shard_map.82
  71.1 0.5 copy-done
  71.6 0.3 collective-permute-start.19
  71.9 0.3 shard_map.83
  72.1 2.8 %collective-permute-start.20 = (s16[128,1664]{1,0:T(8,128)(2,1)S(1)}, s16[128,1664]{1,0:T(8,128)(2,1)S(1)}, u32[]{:S(2)}, u32[]{:S(2)}) collective-permute-start(s16[128,1664]{1,0:T(8,128)(2,1)S(1)} %shard_map.83), channel_id=1, source_target_pairs={{0,14},{1,15},{2,4},{3,5},{4,2},{5,3},{6,8},{7,9},{8,6},{9,7},{10,... | collective-permute-start | bytes 1277960 | tf_op jit(solution)/shard_map/ppermute | solution.py:53
  74.9 0.5 shard_map.86
  75.4 0.1 collective-permute-start.28
  75.5 4.3 %collective-permute-start.29 = (s16[128,1664]{1,0:T(8,128)(2,1)S(1)}, s16[128,1664]{1,0:T(8,128)(2,1)S(1)}, u32[]{:S(2)}, u32[]{:S(2)}) collective-permute-start(s16[128,1664]{1,0:T(8,128)(2,1)S(1)} %get-tuple-element.51.refs_2_), channel_id=1, source_target_pairs={{0,225},{1,224},{2,227},{3,226},{4,229},{5,228},{6,231},{7,230},{8... | collective-permute-start | bytes 1277960 | tf_op jit(solution)/shard_map/ppermute | solution.py:53
  79.7 1.7 %shard_map.87.refs_1_.refs_0_ = f32[384,1536]{1,0:T(8,128)S(1)} custom-call(bf16[1024,1280]{1,0:T(8,128)(2,1)S(1)} %get-tuple-element.45.refs_0_, bf16[1280,1536]{1,0:T(8,128)(2,1)S(1)} %get-tuple-element.37.refs_4_.refs_1_, s16[128,1664]{1,0:T(8,128)(2,1)S(1)} %get-tuple-element.51.refs_2_, f32[8,128]{1,0:T(8,128)S(1)} %collective-permute-done.16.refs_3_.refs_2_), custom_call_target="tpu_custom_call" | custom-call | flops 503316480 | tf_op jit(solution)/shard_map/pallas_call | solution.py:79
  81.4 1.4 %collective-permute-done.19.refs_2_.refs_5_ = s16[128,1664]{1,0:T(8,128)(2,1)S(1)} collective-permute-done((s16[128,1664]{1,0:T(8,128)(2,1)S(1)}, s16[128,1664]{1,0:T(8,128)(2,1)S(1)}, u32[]{:S(2)}, u32[]{:S(2)}) %collective-permute-start.19) | collective-permute-done | bytes 426016 | tf_op jit(solution)/shard_map/ppermute | solution.py:53
  82.8 0.3 shard_map.89.refs_5_
  83.1 0.9 collective-permute-start.23
  84.0 0.4 collective-permute-done.20.refs_2_.refs_6_
  84.4 0.3 shard_map.88.refs_4_
  84.7 0.1 collective-permute-start.22
  84.8 0.5 shard_map.91
  85.3 0.1 collective-permute-start.25
  85.4 0.7 collective-permute-done.28.refs_2_
  86.1 4.2 %collective-permute-start.26 = (s16[128,1664]{1,0:T(8,128)(2,1)S(1)}, s16[128,1664]{1,0:T(8,128)(2,1)S(1)}, u32[]{:S(2)}, u32[]{:S(2)}) collective-permute-start(s16[128,1664]{1,0:T(8,128)(2,1)S(1)} %get-tuple-element.54), channel_id=1, source_target_pairs={{0,225},{1,224},{2,227},{3,226},{4,229},{5,228},{6,231},{7,230},{8... | collective-permute-start | bytes 1277960 | tf_op jit(solution)/shard_map/ppermute | solution.py:53
  90.3 0.4 shard_map.94
  90.7 0.1 collective-permute-start.30
  90.8 3.9 %collective-permute-done.23.refs_8_.refs_2_.refs_3_ = s16[128,1664]{1,0:T(8,128)(2,1)S(1)} collective-permute-done((s16[128,1664]{1,0:T(8,128)(2,1)S(1)}, s16[128,1664]{1,0:T(8,128)(2,1)S(1)}, u32[]{:S(2)}, u32[]{:S(2)}) %collective-permute-start.23) | collective-permute-done | bytes 426016 | tf_op jit(solution)/shard_map/ppermute | solution.py:53
  94.8 0.9 shard_map.98
  95.7 0.2 shard_map.90.refs_9_
  96.0 1.9 %collective-permute-start.32 = (s16[64,1664]{1,0:T(8,128)(2,1)S(1)}, s16[64,1664]{1,0:T(8,128)(2,1)}, u32[]{:S(2)}, u32[]{:S(2)}) collective-permute-start(s16[64,1664]{1,0:T(8,128)(2,1)S(1)} %shard_map.90.refs_9_), channel_id=1, source_target_pairs={{0,14},{1,15},{2,4},{3,5},{4,2},{5,3},{6,8},{7,9},{8,6},{9,7},{10,... | collective-permute-start | bytes 638984 | tf_op jit(solution)/shard_map/ppermute | solution.py:53
  97.8 1.3 %collective-permute-done.26.refs_3_ = s16[128,1664]{1,0:T(8,128)(2,1)S(1)} collective-permute-done((s16[128,1664]{1,0:T(8,128)(2,1)S(1)}, s16[128,1664]{1,0:T(8,128)(2,1)S(1)}, u32[]{:S(2)}, u32[]{:S(2)}) %collective-permute-start.26) | collective-permute-done | bytes 426016 | tf_op jit(solution)/shard_map/ppermute | solution.py:53
  99.1 0.4 shard_map.92.refs_10_.refs_1_
  99.5 0.2 shard_map.93.refs_0_
  99.7 0.1 collective-permute-start.27
  99.8 0.4 collective-permute-done.30.refs_2_
  100.3 1.0 shard_map.95
  101.3 1.5 %collective-permute-done.27.refs_1_ = f32[8,128]{1,0:T(8,128)S(1)} collective-permute-done((f32[8,128]{1,0:T(8,128)S(1)}, f32[8,128]{1,0:T(8,128)S(1)}, u32[]{:S(2)}, u32[]{:S(2)}) %collective-permute-start.27) | collective-permute-done | bytes 4128 | tf_op jit(solution)/shard_map/ppermute | solution.py:53
  102.8 0.6 shard_map.96
  103.4 8.3 %all-to-all-start = ((f32[16,8,128]{2,1,0:T(8,128)}), f32[16,8,128]{2,1,0:T(8,128)S(1)}, u32[]{:S(2)}, u32[]{:S(2)}) async-start(f32[16,8,128]{2,1,0:T(8,128)} %bitcast.2), calls=%async_computation | async-start | bytes 131072 | tf_op jit(solution)/shard_map/all_to_all | solution.py:61
  111.8 2.2 %shard_map.99 = (f32[128,1536]{1,0:T(8,128)}, f32[8,128]{1,0:T(8,128)}) custom-call(f32[1]{0:T(128)S(6)} %copy.20.refs_0_, f32[384,1536]{1,0:T(8,128)S(1)} %shard_map.87.refs_1_.refs_0_, s16[128,1664]{1,0:T(8,128)(2,1)S(1)} %collective-permute-done.22.refs_2_.refs_7_, s16[128,1664]{1,0:T(8,128)(2,1)S(1)} %collective-permute-done.23.refs_8_.refs_2_.refs_3_, ...), custom_call_target="tpu_custom_call" | custom-call | tf_op jit(solution)/shard_map/pallas_call | solution.py:79
  113.9 5.1 %all-to-all-done = f32[16,8,128]{2,1,0:T(8,128)S(1)} async-done(((f32[16,8,128]{2,1,0:T(8,128)}), f32[16,8,128]{2,1,0:T(8,128)S(1)}, u32[]{:S(2)}, u32[]{:S(2)}) %all-to-all-start) | async-done | bytes 65568 | tf_op jit(solution)/shard_map/all_to_all | solution.py:61
  119.1 0.6 shard_map.97
  (38 shorter events, 0.2 us)
Async XLA Ops:
  0.6 38.6 %copy-start.3 = (bf16[128,1536]{1,0:T(8,128)(2,1)S(1)}, bf16[128,1536]{1,0:T(8,128)(2,1)}, u32[]{:S(2)}) copy-start(bf16[128,1536]{1,0:T(8,128)(2,1)} %refs_3_.1) | copy-start | bytes 1179652
  0.6 38.6 %copy-start.2 = (bf16[128,1536]{1,0:T(8,128)(2,1)S(1)}, bf16[128,1536]{1,0:T(8,128)(2,1)}, u32[]{:S(2)}) copy-start(bf16[128,1536]{1,0:T(8,128)(2,1)} %refs_11_.1) | copy-start | bytes 1179652
  0.7 38.6 %copy-start.4 = (s32[128]{0:T(128)S(1)}, s32[128]{0:T(128)}, u32[]{:S(2)}) copy-start(s32[128]{0:T(128)} %param.7) | copy-start | bytes 1540
  0.7 12.6 %collective-permute-start.7 = (bf16[128,1536]{1,0:T(8,128)(2,1)}, bf16[128,1536]{1,0:T(8,128)(2,1)S(1)}, u32[]{:S(2)}, u32[]{:S(2)}) collective-permute-start(bf16[128,1536]{1,0:T(8,128)(2,1)} %refs_3_.1), channel_id=1, source_target_pairs={{0,32},{1,33},{2,34},{3,35},{4,36},{5,37},{6,38},{7,39},{8,40},{9,... | collective-permute-start | bytes 1179656 | tf_op jit(solution)/shard_map/ppermute | solution.py:53
  2.9 12.9 %collective-permute-start.8 = (bf16[128,1536]{1,0:T(8,128)(2,1)}, bf16[128,1536]{1,0:T(8,128)(2,1)S(1)}, u32[]{:S(2)}, u32[]{:S(2)}) collective-permute-start(bf16[128,1536]{1,0:T(8,128)(2,1)} %refs_3_.1), channel_id=1, source_target_pairs={{0,225},{1,224},{2,227},{3,226},{4,229},{5,228},{6,231},{7,230},{8... | collective-permute-start | bytes 1179656 | tf_op jit(solution)/shard_map/ppermute | solution.py:53
  7.0 9.6 %collective-permute-start.6 = (bf16[128,1536]{1,0:T(8,128)(2,1)}, bf16[128,1536]{1,0:T(8,128)(2,1)S(1)}, u32[]{:S(2)}, u32[]{:S(2)}) collective-permute-start(bf16[128,1536]{1,0:T(8,128)(2,1)} %refs_3_.1), channel_id=1, source_target_pairs={{0,1},{1,0},{2,3},{3,2},{4,5},{5,4},{6,7},{7,6},{8,9},{9,8},{10,11... | collective-permute-start | bytes 1179656 | tf_op jit(solution)/shard_map/ppermute | solution.py:53
  7.0 13.3 %collective-permute-start = (bf16[128,1536]{1,0:T(8,128)(2,1)}, bf16[128,1536]{1,0:T(8,128)(2,1)S(1)}, u32[]{:S(2)}, u32[]{:S(2)}) collective-permute-start(bf16[128,1536]{1,0:T(8,128)(2,1)} %refs_11_.1), channel_id=1, source_target_pairs={{0,2},{1,3},{2,0},{3,1},{4,6},{5,7},{6,4},{7,5},{8,10},{9,11},{10,... | collective-permute-start | bytes 1179656 | tf_op jit(solution)/shard_map/ppermute | solution.py:53
  8.6 17.2 %collective-permute-start.3 = (bf16[128,1536]{1,0:T(8,128)(2,1)}, bf16[128,1536]{1,0:T(8,128)(2,1)S(1)}, u32[]{:S(2)}, u32[]{:S(2)}) collective-permute-start(bf16[128,1536]{1,0:T(8,128)(2,1)} %refs_11_.1), channel_id=1, source_target_pairs={{0,14},{1,15},{2,4},{3,5},{4,2},{5,3},{6,8},{7,9},{8,6},{9,7},{10,... | collective-permute-start | bytes 1179656 | tf_op jit(solution)/shard_map/ppermute | solution.py:53
  16.6 11.7 %collective-permute-start.11 = (bf16[128,1536]{1,0:T(8,128)(2,1)S(1)}, bf16[128,1536]{1,0:T(8,128)(2,1)S(1)}, u32[]{:S(2)}, u32[]{:S(2)}) collective-permute-start(bf16[128,1536]{1,0:T(8,128)(2,1)S(1)} %shard_map.76.refs_4_), channel_id=1, source_target_pairs={{0,32},{1,33},{2,34},{3,35},{4,36},{5,37},{6,38},{7,39},{8,40},{9,... | collective-permute-start | bytes 1179656 | tf_op jit(solution)/shard_map/ppermute | solution.py:53
  16.6 11.8 %collective-permute-start.12 = (bf16[128,1536]{1,0:T(8,128)(2,1)S(1)}, bf16[128,1536]{1,0:T(8,128)(2,1)S(1)}, u32[]{:S(2)}, u32[]{:S(2)}) collective-permute-start(bf16[128,1536]{1,0:T(8,128)(2,1)S(1)} %shard_map.76.refs_4_), channel_id=1, source_target_pairs={{0,225},{1,224},{2,227},{3,226},{4,229},{5,228},{6,231},{7,230},{8... | collective-permute-start | bytes 1179656 | tf_op jit(solution)/shard_map/ppermute | solution.py:53
  20.3 13.0 %collective-permute-start.1 = (bf16[128,1536]{1,0:T(8,128)(2,1)S(1)}, bf16[128,1536]{1,0:T(8,128)(2,1)}, u32[]{:S(2)}, u32[]{:S(2)}) collective-permute-start(bf16[128,1536]{1,0:T(8,128)(2,1)S(1)} %collective-permute-done.refs_12_), channel_id=1, source_target_pairs={{0,14},{1,15},{2,4},{3,5},{4,2},{5,3},{6,8},{7,9},{8,6},{9,7},{10,... | collective-permute-start | bytes 1179656 | tf_op jit(solution)/shard_map/ppermute | solution.py:53
  25.8 8.3 %collective-permute-start.4 = (bf16[128,1536]{1,0:T(8,128)(2,1)S(1)}, bf16[128,1536]{1,0:T(8,128)(2,1)}, u32[]{:S(2)}, u32[]{:S(2)}) collective-permute-start(bf16[128,1536]{1,0:T(8,128)(2,1)S(1)} %collective-permute-done.3.refs_13_), channel_id=1, source_target_pairs={{0,2},{1,3},{2,0},{3,1},{4,6},{5,7},{6,4},{7,5},{8,10},{9,11},{10,... | collective-permute-start | bytes 1179656 | tf_op jit(solution)/shard_map/ppermute | solution.py:53
  25.8 13.3 %collective-permute-start.9 = (bf16[128,1536]{1,0:T(8,128)(2,1)}, bf16[128,1536]{1,0:T(8,128)(2,1)}, u32[]{:S(2)}, u32[]{:S(2)}) collective-permute-start(bf16[128,1536]{1,0:T(8,128)(2,1)} %refs_3_.1), channel_id=1, source_target_pairs={{0,16},{1,17},{2,18},{3,19},{4,20},{5,21},{6,22},{7,23},{8,24},{9,... | collective-permute-start | bytes 1179656 | tf_op jit(solution)/shard_map/ppermute | solution.py:53
  28.3 10.9 %collective-permute-start.10 = (bf16[128,1536]{1,0:T(8,128)(2,1)S(1)}, bf16[128,1536]{1,0:T(8,128)(2,1)}, u32[]{:S(2)}, u32[]{:S(2)}) collective-permute-start(bf16[128,1536]{1,0:T(8,128)(2,1)S(1)} %shard_map.76.refs_4_), channel_id=1, source_target_pairs={{0,16},{1,17},{2,18},{3,19},{4,20},{5,21},{6,22},{7,23},{8,24},{9,... | collective-permute-start | bytes 1179656 | tf_op jit(solution)/shard_map/ppermute | solution.py:53
  28.4 21.1 %collective-permute-start.15 = (bf16[256,1536]{1,0:T(8,128)(2,1)S(1)}, bf16[256,1536]{1,0:T(8,128)(2,1)S(1)}, u32[]{:S(2)}, u32[]{:S(2)}) collective-permute-start(bf16[256,1536]{1,0:T(8,128)(2,1)S(1)} %shard_map.79), channel_id=1, source_target_pairs={{0,16},{1,17},{2,18},{3,19},{4,20},{5,21},{6,22},{7,23},{8,24},{9,... | collective-permute-start | bytes 2359304 | tf_op jit(solution)/shard_map/ppermute | solution.py:53
  33.2 11.3 %collective-permute-start.2 = (bf16[128,1536]{1,0:T(8,128)(2,1)}, bf16[128,1536]{1,0:T(8,128)(2,1)S(1)}, u32[]{:S(2)}, u32[]{:S(2)}) collective-permute-start(bf16[128,1536]{1,0:T(8,128)(2,1)} %collective-permute-done.1.refs_15_), channel_id=1, source_target_pairs={{0,2},{1,3},{2,0},{3,1},{4,6},{5,7},{6,4},{7,5},{8,10},{9,11},{10,... | collective-permute-start | bytes 1179656 | tf_op jit(solution)/shard_map/ppermute | solution.py:53
  34.1 11.7 %collective-permute-start.5 = (bf16[128,1536]{1,0:T(8,128)(2,1)}, bf16[128,1536]{1,0:T(8,128)(2,1)S(1)}, u32[]{:S(2)}, u32[]{:S(2)}) collective-permute-start(bf16[128,1536]{1,0:T(8,128)(2,1)} %collective-permute-done.4.refs_14_), channel_id=1, source_target_pairs={{0,14},{1,15},{2,4},{3,5},{4,2},{5,3},{6,8},{7,9},{8,6},{9,7},{10,... | collective-permute-start | bytes 1179656 | tf_op jit(solution)/shard_map/ppermute | solution.py:53
  45.8 6.5 %collective-permute-start.13 = (bf16[64,1536]{1,0:T(8,128)(2,1)S(1)}, bf16[64,1536]{1,0:T(8,128)(2,1)S(1)}, u32[]{:S(2)}, u32[]{:S(2)}) collective-permute-start(bf16[64,1536]{1,0:T(8,128)(2,1)S(1)} %get-tuple-element.32), channel_id=1, source_target_pairs={{0,2},{1,3},{2,0},{3,1},{4,6},{5,7},{6,4},{7,5},{8,10},{9,11},{10,... | collective-permute-start | bytes 589832 | tf_op jit(solution)/shard_map/ppermute | solution.py:53
  46.1 6.5 %collective-permute-start.14 = (bf16[64,1536]{1,0:T(8,128)(2,1)S(1)}, bf16[64,1536]{1,0:T(8,128)(2,1)S(1)}, u32[]{:S(2)}, u32[]{:S(2)}) collective-permute-start(bf16[64,1536]{1,0:T(8,128)(2,1)S(1)} %get-tuple-element.33), channel_id=1, source_target_pairs={{0,14},{1,15},{2,4},{3,5},{4,2},{5,3},{6,8},{7,9},{8,6},{9,7},{10,... | collective-permute-start | bytes 589832 | tf_op jit(solution)/shard_map/ppermute | solution.py:53
  56.9 13.9 %collective-permute-start.18 = (s16[128,1664]{1,0:T(8,128)(2,1)S(1)}, s16[128,1664]{1,0:T(8,128)(2,1)S(1)}, u32[]{:S(2)}, u32[]{:S(2)}) collective-permute-start(s16[128,1664]{1,0:T(8,128)(2,1)S(1)} %get-tuple-element.43), channel_id=1, source_target_pairs={{0,14},{1,15},{2,4},{3,5},{4,2},{5,3},{6,8},{7,9},{8,6},{9,7},{10,... | collective-permute-start | bytes 1277960 | tf_op jit(solution)/shard_map/ppermute | solution.py:53
  59.7 12.2 %collective-permute-start.17 = (s16[128,1664]{1,0:T(8,128)(2,1)S(1)}, s16[128,1664]{1,0:T(8,128)(2,1)S(1)}, u32[]{:S(2)}, u32[]{:S(2)}) collective-permute-start(s16[128,1664]{1,0:T(8,128)(2,1)S(1)} %get-tuple-element.42.refs_2_), channel_id=1, source_target_pairs={{0,2},{1,3},{2,0},{3,1},{4,6},{5,7},{6,4},{7,5},{8,10},{9,11},{10,... | collective-permute-start | bytes 1277960 | tf_op jit(solution)/shard_map/ppermute | solution.py:53
  61.8 13.2 %collective-permute-start.21 = (s16[256,1664]{1,0:T(8,128)(2,1)S(1)}, s16[256,1664]{1,0:T(8,128)(2,1)S(1)}, u32[]{:S(2)}, u32[]{:S(2)}) collective-permute-start(s16[256,1664]{1,0:T(8,128)(2,1)S(1)} %get-tuple-element.50), channel_id=1, source_target_pairs={{0,16},{1,17},{2,18},{3,19},{4,20},{5,21},{6,22},{7,23},{8,24},{9,... | collective-permute-start | bytes 2555912 | tf_op jit(solution)/shard_map/ppermute | solution.py:53
  65.0 10.5 %collective-permute-start.16 = (f32[8,128]{1,0:T(8,128)S(1)}, f32[8,128]{1,0:T(8,128)S(1)}, u32[]{:S(2)}, u32[]{:S(2)}) collective-permute-start(f32[8,128]{1,0:T(8,128)S(1)} %get-tuple-element.41.refs_1_), channel_id=1, source_target_pairs={{0,8},{1,9},{2,10},{3,11},{4,12},{5,13},{6,14},{7,15},{8,0},{9,1},... | collective-permute-start | bytes 12296 | tf_op jit(solution)/shard_map/ppermute | solution.py:53
  67.8 17.0 %collective-permute-start.24 = (s16[256,1664]{1,0:T(8,128)(2,1)S(1)}, s16[256,1664]{1,0:T(8,128)(2,1)S(1)}, u32[]{:S(2)}, u32[]{:S(2)}) collective-permute-start(s16[256,1664]{1,0:T(8,128)(2,1)S(1)} %get-tuple-element.47.refs_2_), channel_id=1, source_target_pairs={{0,16},{1,17},{2,18},{3,19},{4,20},{5,21},{6,22},{7,23},{8,24},{9,... | collective-permute-start | bytes 2555912 | tf_op jit(solution)/shard_map/ppermute | solution.py:53
  70.8 0.8 copy-start
  71.6 11.3 %collective-permute-start.19 = (s16[128,1664]{1,0:T(8,128)(2,1)S(1)}, s16[128,1664]{1,0:T(8,128)(2,1)S(1)}, u32[]{:S(2)}, u32[]{:S(2)}) collective-permute-start(s16[128,1664]{1,0:T(8,128)(2,1)S(1)} %shard_map.82), channel_id=1, source_target_pairs={{0,2},{1,3},{2,0},{3,1},{4,6},{5,7},{6,4},{7,5},{8,10},{9,11},{10,... | collective-permute-start | bytes 1277960 | tf_op jit(solution)/shard_map/ppermute | solution.py:53
  72.1 12.3 %collective-permute-start.20 = (s16[128,1664]{1,0:T(8,128)(2,1)S(1)}, s16[128,1664]{1,0:T(8,128)(2,1)S(1)}, u32[]{:S(2)}, u32[]{:S(2)}) collective-permute-start(s16[128,1664]{1,0:T(8,128)(2,1)S(1)} %shard_map.83), channel_id=1, source_target_pairs={{0,14},{1,15},{2,4},{3,5},{4,2},{5,3},{6,8},{7,9},{8,6},{9,7},{10,... | collective-permute-start | bytes 1277960 | tf_op jit(solution)/shard_map/ppermute | solution.py:53
  75.4 10.7 %collective-permute-start.28 = (s16[128,1664]{1,0:T(8,128)(2,1)S(1)}, s16[128,1664]{1,0:T(8,128)(2,1)S(1)}, u32[]{:S(2)}, u32[]{:S(2)}) collective-permute-start(s16[128,1664]{1,0:T(8,128)(2,1)S(1)} %get-tuple-element.55), channel_id=1, source_target_pairs={{0,32},{1,33},{2,34},{3,35},{4,36},{5,37},{6,38},{7,39},{8,40},{9,... | collective-permute-start | bytes 1277960 | tf_op jit(solution)/shard_map/ppermute | solution.py:53
  75.5 14.8 %collective-permute-start.29 = (s16[128,1664]{1,0:T(8,128)(2,1)S(1)}, s16[128,1664]{1,0:T(8,128)(2,1)S(1)}, u32[]{:S(2)}, u32[]{:S(2)}) collective-permute-start(s16[128,1664]{1,0:T(8,128)(2,1)S(1)} %get-tuple-element.51.refs_2_), channel_id=1, source_target_pairs={{0,225},{1,224},{2,227},{3,226},{4,229},{5,228},{6,231},{7,230},{8... | collective-permute-start | bytes 1277960 | tf_op jit(solution)/shard_map/ppermute | solution.py:53
  83.1 11.7 %collective-permute-start.23 = (s16[128,1664]{1,0:T(8,128)(2,1)S(1)}, s16[128,1664]{1,0:T(8,128)(2,1)S(1)}, u32[]{:S(2)}, u32[]{:S(2)}) collective-permute-start(s16[128,1664]{1,0:T(8,128)(2,1)S(1)} %shard_map.89.refs_5_), channel_id=1, source_target_pairs={{0,14},{1,15},{2,4},{3,5},{4,2},{5,3},{6,8},{7,9},{8,6},{9,7},{10,... | collective-permute-start | bytes 1277960 | tf_op jit(solution)/shard_map/ppermute | solution.py:53
  84.7 11.0 %collective-permute-start.22 = (s16[128,1664]{1,0:T(8,128)(2,1)S(1)}, s16[128,1664]{1,0:T(8,128)(2,1)S(1)}, u32[]{:S(2)}, u32[]{:S(2)}) collective-permute-start(s16[128,1664]{1,0:T(8,128)(2,1)S(1)} %shard_map.88.refs_4_), channel_id=1, source_target_pairs={{0,2},{1,3},{2,0},{3,1},{4,6},{5,7},{6,4},{7,5},{8,10},{9,11},{10,... | collective-permute-start | bytes 1277960 | tf_op jit(solution)/shard_map/ppermute | solution.py:53
  85.3 12.5 %collective-permute-start.25 = (s16[128,1664]{1,0:T(8,128)(2,1)S(1)}, s16[128,1664]{1,0:T(8,128)(2,1)S(1)}, u32[]{:S(2)}, u32[]{:S(2)}) collective-permute-start(s16[128,1664]{1,0:T(8,128)(2,1)S(1)} %get-tuple-element.53), channel_id=1, source_target_pairs={{0,32},{1,33},{2,34},{3,35},{4,36},{5,37},{6,38},{7,39},{8,40},{9,... | collective-permute-start | bytes 1277960 | tf_op jit(solution)/shard_map/ppermute | solution.py:53
  86.1 13.0 %collective-permute-start.26 = (s16[128,1664]{1,0:T(8,128)(2,1)S(1)}, s16[128,1664]{1,0:T(8,128)(2,1)S(1)}, u32[]{:S(2)}, u32[]{:S(2)}) collective-permute-start(s16[128,1664]{1,0:T(8,128)(2,1)S(1)} %get-tuple-element.54), channel_id=1, source_target_pairs={{0,225},{1,224},{2,227},{3,226},{4,229},{5,228},{6,231},{7,230},{8... | collective-permute-start | bytes 1277960 | tf_op jit(solution)/shard_map/ppermute | solution.py:53
  90.7 9.5 %collective-permute-start.30 = (s16[128,1664]{1,0:T(8,128)(2,1)S(1)}, s16[128,1664]{1,0:T(8,128)(2,1)S(1)}, u32[]{:S(2)}, u32[]{:S(2)}) collective-permute-start(s16[128,1664]{1,0:T(8,128)(2,1)S(1)} %shard_map.94), channel_id=1, source_target_pairs={{0,1},{1,0},{2,3},{3,2},{4,5},{5,4},{6,7},{7,6},{8,9},{9,8},{10,11... | collective-permute-start | bytes 1277960 | tf_op jit(solution)/shard_map/ppermute | solution.py:53
  95.7 16.0 %collective-permute-start.31 = (s16[64,1664]{1,0:T(8,128)(2,1)}, s16[64,1664]{1,0:T(8,128)(2,1)}, u32[]{:S(2)}, u32[]{:S(2)}) collective-permute-start(s16[64,1664]{1,0:T(8,128)(2,1)} %shard_map.98), channel_id=1, source_target_pairs={{0,2},{1,3},{2,0},{3,1},{4,6},{5,7},{6,4},{7,5},{8,10},{9,11},{10,... | collective-permute-start | bytes 638984 | tf_op jit(solution)/shard_map/ppermute | solution.py:53
  95.9 3.6 %copy-start.1 = (s16[128,1664]{1,0:T(8,128)(2,1)S(1)}, s16[128,1664]{1,0:T(8,128)(2,1)}, u32[]{:S(2)}) copy-start(s16[128,1664]{1,0:T(8,128)(2,1)} %copy-done) | copy-start | bytes 1277956
  96.0 15.8 %collective-permute-start.32 = (s16[64,1664]{1,0:T(8,128)(2,1)S(1)}, s16[64,1664]{1,0:T(8,128)(2,1)}, u32[]{:S(2)}, u32[]{:S(2)}) collective-permute-start(s16[64,1664]{1,0:T(8,128)(2,1)S(1)} %shard_map.90.refs_9_), channel_id=1, source_target_pairs={{0,14},{1,15},{2,4},{3,5},{4,2},{5,3},{6,8},{7,9},{8,6},{9,7},{10,... | collective-permute-start | bytes 638984 | tf_op jit(solution)/shard_map/ppermute | solution.py:53
  99.7 3.1 %collective-permute-start.27 = (f32[8,128]{1,0:T(8,128)S(1)}, f32[8,128]{1,0:T(8,128)S(1)}, u32[]{:S(2)}, u32[]{:S(2)}) collective-permute-start(f32[8,128]{1,0:T(8,128)S(1)} %shard_map.93.refs_0_), channel_id=1, source_target_pairs={{0,1},{1,0},{2,3},{3,2},{4,5},{5,4},{6,7},{7,6},{8,9},{9,8},{10,11... | collective-permute-start | bytes 12296 | tf_op jit(solution)/shard_map/ppermute | solution.py:53
  103.4 15.7 %all-to-all-start = ((f32[16,8,128]{2,1,0:T(8,128)}), f32[16,8,128]{2,1,0:T(8,128)S(1)}, u32[]{:S(2)}, u32[]{:S(2)}) async-start(f32[16,8,128]{2,1,0:T(8,128)} %bitcast.2), calls=%async_computation | async-start | bytes 131072 | tf_op jit(solution)/shard_map/all_to_all | solution.py:61
